TPU v7x, 32 devices: a whole 2x2x4 slice. The times are simulated.
32 devices in a mesh: dp: 4 (over z), row: 4 (over x, core), col: 2 (over y).
Axes of the slice: x: 2, y: 2, z: 4, core: 2. Of those that a mesh axis runs over, the one named last changes fastest.
Arguments:
- activations: bfloat16 [4096, 18432], P(('dp', 'col'), 'row'), may hold values from -6 to 6
- cotangent: bfloat16 [4096, 16384], P(('dp', 'row'), 'col'), may hold values from -0.09375 to 0.09375
- weight: float32 [18432, 16384], P(('row', 'dp'), 'col'), may hold values from -60 to 60
- row_moment: float32 [18432], P(('row', 'dp')), may hold values from 0.05 to 1
- col_moment: float32 [16384], P('col'), may hold values from 0.05 to 1
Outputs:
- new_weight: float32 [18432, 16384], P(('row', 'dp'), 'col')
- clipped_update: bfloat16 [18432, 16384], P(('row', 'dp'), 'col')
- new_row_moment: float32 [18432], P(('row', 'dp'))
- new_col_moment: float32 [16384], P('col')
All inputs are finite; a program needn't handle non-finite values.
Results may differ from a plain program's by a relative error of at most 0.001.
Values may be sent and summed in bfloat16 or wider, within the bound.
No kernel may reach another device: no remote copies, remote signals or barrier semaphores. Data moves between devices by JAX's collectives and lax.ppermute only.
A program may use at most 384 MiB of HBM per device.

v0:
```python
import jax
import jax.numpy as jnp
from jax import lax
from jax.sharding import PartitionSpec as P

D = 18432
F = 16384
STEP = 10


def token_product(left, right):
    return lax.dot_general(
        left, right, (((0,), (0,)), ((), ())), preferred_element_type=jnp.float32
    )


def body(activations, cotangent, weight, row_moment, col_moment):
    decay_rate = 1.0 - float(STEP) ** (-0.8)
    relative = min(0.01, float(STEP) ** (-0.5))
    act_rows = lax.all_gather(activations, "col", axis=0, tiled=True)
    cot_rows = lax.all_gather(cotangent, "row", axis=0, tiled=True)
    gradient = lax.psum_scatter(
        token_product(act_rows, cot_rows), "dp", scatter_dimension=0, tiled=True
    )
    squared = gradient * gradient
    row_sum = lax.psum(jnp.sum(squared, axis=1), "col")
    col_sum = lax.psum(jnp.sum(squared, axis=0), ("dp", "row"))
    row_new = decay_rate * row_moment + (1.0 - decay_rate) * row_sum / F
    col_new = decay_rate * col_moment + (1.0 - decay_rate) * col_sum / D
    update = gradient * lax.rsqrt(row_new)[:, None] * lax.rsqrt(col_new)[None, :]
    update_total = lax.psum(jnp.sum(update * update), ("dp", "row", "col"))
    clip_factor = jnp.maximum(1.0, jnp.sqrt(update_total / (D * F)))
    clipped = update / clip_factor
    new_weight = weight - relative * clipped
    return (new_weight, clipped.astype(jnp.bfloat16), row_new, col_new)


def solution(mesh):
    placed = (
        P(("dp", "col"), "row"),
        P(("dp", "row"), "col"),
        P(("row", "dp"), "col"),
        P(("row", "dp")),
        P("col"),
    )
    return jax.shard_map(
        body,
        mesh=mesh,
        in_specs=placed,
        out_specs=(P(("row", "dp"), "col"), P(("row", "dp"), "col"), P(("row", "dp")), P("col")),
        check_vma=False,
    )
```

profile of v0, /device:TPU:0, one launch (start us, length us, event | category | flops | bytes accessed | tf_op | source)
XLA Modules:
  0.0 2963.3 jit_solution(16257239249341692400)
XLA Ops:
  7.2 0.0 all-gather.3.cloned.1.call-start
  7.2 0.7 all-gather.3.cloned.1.call-update
  7.9 0.0 all-gather.5.cloned.1.call-start
  7.9 0.7 all-gather.5.cloned.1.call-update
  8.6 0.0 reduce-scatter.2.cloned.1.call-start
  8.7 121.6 %all-gather.3.cloned.1.call-done = bf16[1024,4608]{1,0:T(8,128)(2,1)} async-done(((bf16[512,4608]{1,0:T(8,128)(2,1)}), bf16[1024,4608]{1,0:T(8,128)(2,1)}) %all-gather.3.cloned.1.call-update) | async-done | bytes 9437200 | tf_op jit(solution)/shard_map/all_gather | solution.py:20
  130.3 107.5 %all-gather.5.cloned.1.call-done = bf16[1024,8192]{1,0:T(8,128)(2,1)} async-done(((bf16[256,8192]{1,0:T(8,128)(2,1)}), bf16[1024,8192]{1,0:T(8,128)(2,1)}) %all-gather.5.cloned.1.call-update) | async-done | bytes 16777232 | tf_op jit(solution)/shard_map/all_gather | solution.py:21
  237.8 90.9 %fusion.4 = f32[4608,8192]{1,0:T(8,128)} fusion(bf16[1024,4608]{1,0:T(8,128)(2,1)} %all-gather.3.cloned.1.call-done, bf16[1024,8192]{1,0:T(8,128)(2,1)} %all-gather.5.cloned.1.call-done), kind=kOutput, calls=%fused_computation.11 | convolution fusion | flops 77309411328 | bytes 177209344 | tf_op jit(solution)/shard_map/dot_general | solution.py:12
  328.7 0.0 reduce-scatter.2.cloned.1.call-update
  328.7 0.0 copy-start.1
  328.8 0.0 copy-start
  328.8 2446.5 %reduce-scatter.2.cloned.1.call-done = f32[1152,8192]{1,0:T(8,128)} async-done(((f32[4608,8192]{1,0:T(8,128)}), f32[1152,8192]{1,0:T(8,128)}) %reduce-scatter.2.cloned.1.call-update) | async-done | bytes 37748752 | tf_op jit(solution)/shard_map/reduce_scatter | solution.py:22
  2775.2 14.3 multiply_reduce_fusion.2
  2789.5 5.0 psum.21
  2794.5 61.0 %psum.22 = f32[8192]{0:T(1024)S(1)} all-reduce(f32[8192]{0:T(1024)S(1)} %get-tuple-element.5), channel_id=1, replica_groups=mesh['dp'=4,'row'=4,'col'=2] {'dp','row'}, use_global_device_ids=true, to_apply=%region_4.0 | all-reduce | flops 8192 | bytes 65536 | tf_op jit(solution)/shard_map/psum | solution.py:27
  2855.5 0.0 copy-done.1
  2855.5 0.6 fusion.2
  2856.1 0.0 copy-done
  2856.1 0.6 fusion.3
  2856.7 17.8 multiply_reduce_fusion
  2874.5 37.1 %psum.23 = f32[]{:T(128)} all-reduce(f32[]{:T(128)} %multiply_reduce_fusion), channel_id=1, replica_groups=mesh['dp'=4,'row'=4,'col'=2] {'dp','row','col'}, use_global_device_ids=true, to_apply=%region_6.0 | all-reduce | flops 1 | bytes 8 | tf_op jit(solution)/shard_map/psum | solution.py:31
  2912.3 44.5 %fusion.1 = (bf16[1152,8192]{1,0:T(8,128)(2,1)}, f32[1152,8192]{1,0:T(8,128)}) fusion(f32[]{:T(128)S(6)} %max_shard_map.3, f32[8192]{0:T(1024)S(1)} %get-tuple-element.8, f32[1152,8192]{1,0:T(8,128)} %reduce-scatter.2.cloned.1.call-done, f32[1152]{0:T(1024)S(1)} %get-tuple-element.6, f32[1152,8192]{1,0:T(8,128)} %param.7), kind=kLoop, calls=%fused_computation.6 | loop fusion | flops 56623104 | bytes 132157952 | tf_op jit(solution)/shard_map/convert_element_type | solution.py:35
Async XLA Ops:
  7.2 123.1 %all-gather.3.cloned.1.call-start = ((), (), s32[]{:S(2)}) async-start(), calls=%async_computation.1 | async-start | bytes 14155776 | tf_op jit(solution)/shard_map/all_gather | solution.py:20
  7.9 229.9 %all-gather.5.cloned.1.call-start = ((), (), s32[]{:S(2)}) async-start(), calls=%async_computation.2 | async-start | bytes 20971520 | tf_op jit(solution)/shard_map/all_gather | solution.py:21
  8.6 2766.6 %reduce-scatter.2.cloned.1.call-start = ((), (), s32[]{:S(2)}) async-start(), calls=%async_computation.3 | async-start | bytes 188743680 | tf_op jit(solution)/shard_map/reduce_scatter | solution.py:22
  328.7 2526.8 %copy-start.1 = (f32[1152]{0:T(1024)S(1)}, f32[1152]{0:T(1024)}, u32[]{:S(2)}) copy-start(f32[1152]{0:T(1024)} %param.8) | copy-start | bytes 13828
  328.8 2527.4 %copy-start = (f32[8192]{0:T(1024)S(1)}, f32[8192]{0:T(1024)}, u32[]{:S(2)}) copy-start(f32[8192]{0:T(1024)} %param.9) | copy-start | bytes 98308
Sparse Core Ops, SparseCore 0:
  9.6 120.6 all-gather.2
  131.9 105.9 all-gather.4
  328.9 2446.3 reduce-scatter.1
where the time goes:
time: 2960 us
  waiting for transfers between devices  2680 us (91%)
  blocking collectives  103 us (3%)
  matrix products  90.9 us (3%)
  other arithmetic  77.8 us (3%)
    reduce_scatter x1, waiting for transfers between devices, body(): lax.psum_scatter(token_product(act_rows, cot_rows), 'dp', scatter_dimensi...  2450 us
    all_gather x1, waiting for transfers between devices, body(): act_rows = lax.all_gather(activations, 'col', axis=0, tiled=True)  122 us
    all_gather x1, waiting for transfers between devices, body(): cot_rows = lax.all_gather(cotangent, 'row', axis=0, tiled=True)  108 us
    dot_general x1, matrix products, token_product(): lax.dot_general(left, right, (((0,), (0,)), ((), ())), preferred_element_...  90.9 us
    psum x1, blocking collectives, body(): col_sum = lax.psum(jnp.sum(squared, axis=0), ('dp', 'row'))  61 us
  transfers between devices with their start and end apart: 3, of which 3 were waited for; matrix products, arithmetic and copies ran while one was open for 0% of the time, Pallas kernels for 0%

commit v1 on v0

v1 whole, which is shorter than its diff:
```python
import functools

import jax
import jax.numpy as jnp
from jax import lax
from jax.experimental import pallas as pl
from jax.experimental.pallas import tpu as pltpu
from jax.sharding import PartitionSpec as P

D = 18432
F = 16384
STEP = 10
CHUNKS = 8


def product_kernel(count, act_ref, *refs):
    blocks, (grad_ref, row_ref, col_ref, held) = refs[:count], refs[count:]
    depth = blocks[0].shape[0]
    for k, block in enumerate(blocks):
        held[k * depth : (k + 1) * depth, :] = block[...]
    grad = jnp.dot(act_ref[...], held[...], preferred_element_type=jnp.float32)
    grad_ref[...] = grad
    squared = grad * grad
    col_ref[...] = jnp.sum(squared, axis=0, keepdims=True)
    lanes = squared[:, :128]
    for at in range(128, squared.shape[1], 128):
        lanes = lanes + squared[:, at : at + 128]

    @pl.when(pl.program_id(0) == 0)
    def _():
        row_ref[...] = jnp.zeros_like(row_ref)

    row_ref[...] += lanes


def product(act, blocks):
    rows, tokens = act.shape
    depth, width = blocks[0].shape
    tile = min(256, width)
    return pl.pallas_call(
        functools.partial(product_kernel, len(blocks)),
        grid=(width // tile,),
        in_specs=[pl.BlockSpec((rows, tokens), lambda j: (0, 0))]
        + [pl.BlockSpec((depth, tile), lambda j: (0, j)) for _ in blocks],
        out_specs=[
            pl.BlockSpec((rows, tile), lambda j: (0, j)),
            pl.BlockSpec((rows, 128), lambda j: (0, 0)),
            pl.BlockSpec((1, tile), lambda j: (0, j)),
        ],
        out_shape=[
            jax.ShapeDtypeStruct((rows, width), jnp.float32),
            jax.ShapeDtypeStruct((rows, 128), jnp.float32),
            jax.ShapeDtypeStruct((1, width), jnp.float32),
        ],
        scratch_shapes=[pltpu.VMEM((tokens, tile), jnp.bfloat16)],
        cost_estimate=pl.CostEstimate(
            flops=2 * rows * tokens * width,
            bytes_accessed=2 * (rows + width) * tokens + 4 * rows * width,
            transcendentals=0,
        ),
        compiler_params=pltpu.CompilerParams(vmem_limit_bytes=48 * 2**20),
        name="product",
    )(act, *blocks)


def step_kernel(count, relative, clip_ref, row_ref, col_ref, weight_ref, *refs):
    grads, (new_ref, clipped_ref) = refs[:count], refs[count:]
    for k in range(count):

        @pl.when(pl.program_id(0) == k)
        def _(grad_ref=grads[k]):
            clipped = grad_ref[...] * (row_ref[...] * clip_ref[0, 0]) * col_ref[...]
            new_ref[...] = weight_ref[...] - relative * clipped
            clipped_ref[...] = clipped.astype(jnp.bfloat16)


def weight_step(relative, inverse_clip, row_scale, col_scale, weight, grads):
    rows, columns = weight.shape
    width = grads[0].shape[1]
    count = len(grads)
    tile = 128
    steps = rows // tile

    def own(k):
        return lambda c, i: (jnp.where(c == k, i, jnp.where(c < k, 0, steps - 1)), 0)

    return pl.pallas_call(
        functools.partial(step_kernel, count, relative),
        grid=(count, steps),
        in_specs=[
            pl.BlockSpec(memory_space=pltpu.SMEM),
            pl.BlockSpec((tile, 1), lambda c, i: (i, 0)),
            pl.BlockSpec((1, width), lambda c, i: (0, c)),
            pl.BlockSpec((tile, width), lambda c, i: (i, c)),
        ]
        + [pl.BlockSpec((tile, width), own(k)) for k in range(count)],
        out_specs=[
            pl.BlockSpec((tile, width), lambda c, i: (i, c)),
            pl.BlockSpec((tile, width), lambda c, i: (i, c)),
        ],
        out_shape=[
            jax.ShapeDtypeStruct((rows, columns), jnp.float32),
            jax.ShapeDtypeStruct((rows, columns), jnp.bfloat16),
        ],
        cost_estimate=pl.CostEstimate(
            flops=5 * rows * columns, bytes_accessed=14 * rows * columns, transcendentals=0
        ),
        compiler_params=pltpu.CompilerParams(vmem_limit_bytes=48 * 2**20),
        name="weight_step",
    )(inverse_clip.reshape(1, 1), row_scale[:, None], col_scale[None, :], weight, *grads)


def shifted(value, axis, size, by):
    return lax.ppermute(value, axis, [(i, (i + by) % size) for i in range(size)])


def flipped(value, axis, size, bit):
    return lax.ppermute(value, axis, [(i, i ^ bit) for i in range(size)])


def total(value, axis, size):
    if size & (size - 1):
        return lax.psum(value, axis)
    bit = 1
    while bit < size:
        value = value + flipped(value, axis, size, bit)
        bit *= 2
    return value


def body(sizes, activations, cotangent, weight, row_moment, col_moment):
    n_dp, n_row, n_col = sizes
    z, r, y = lax.axis_index("dp"), lax.axis_index("row"), lax.axis_index("col")
    decay_rate = 1.0 - float(STEP) ** (-0.8)
    relative = min(0.01, float(STEP) ** (-0.5))
    rows = weight.shape[0]
    depth, columns = cotangent.shape
    width = columns // CHUNKS

    held = []
    for s in range(n_dp):
        to = lax.rem(z + s, n_dp)
        piece = lax.dynamic_slice_in_dim(activations, to * rows, rows, axis=1)
        held.append(shifted(piece, "dp", n_dp, s) if s else piece)
    act = []
    for piece in held:
        parts = jnp.zeros((n_col,) + piece.shape, piece.dtype)
        for t in range(n_col):
            part = shifted(piece, "col", n_col, t) if t else piece
            parts = lax.dynamic_update_index_in_dim(parts, part, lax.rem(y - t + n_col, n_col), 0)
        parts = parts.reshape(n_row, depth, rows)
        for u in range(n_row // 2):
            for v in range(2):
                at = lax.rem(r - 2 * u + n_row, n_row) ^ v
                act.append(lax.dynamic_index_in_dim(parts, at, 0, keepdims=False))
    act = jnp.concatenate(act, axis=0).T

    grads, row_lanes, col_new, weighted = [], 0.0, [], 0.0
    for k in range(CHUNKS):
        block = cotangent[:, k * width : (k + 1) * width]
        blocks = []
        for s in range(n_dp):
            if s:
                block = shifted(block, "dp", n_dp, 1)
            for u in range(n_row // 2):
                across = shifted(block, "row", n_row, 2 * u) if u else block
                blocks += [across, flipped(across, "row", n_row, 1)]
        grad, row_part, col_part = product(act, blocks)
        col_sum = total(total(col_part[0], "row", n_row), "dp", n_dp)
        moment = decay_rate * col_moment[k * width : (k + 1) * width] + (1.0 - decay_rate) * col_sum / D
        grads.append(grad)
        row_lanes = row_lanes + row_part
        col_new.append(moment)
        weighted = weighted + jnp.sum(grad * grad * (1.0 / moment)[None, :], axis=1)
    row_sum = jnp.sum(row_lanes, axis=1)
    row_sum, weighted = total(jnp.stack([row_sum, weighted]), "col", n_col)
    row_new = decay_rate * row_moment + (1.0 - decay_rate) * row_sum / F
    col_new = jnp.concatenate(col_new)
    update_total = jnp.sum(weighted / row_new).reshape(1, 1)
    update_total = total(total(update_total, "row", n_row), "dp", n_dp)[0, 0]
    clip_factor = jnp.maximum(1.0, jnp.sqrt(update_total / (D * F)))
    new_weight, clipped = weight_step(
        relative, 1.0 / clip_factor, lax.rsqrt(row_new), lax.rsqrt(col_new), weight, grads
    )
    return (new_weight, clipped, row_new, col_new)


def solution(mesh):
    placed = (
        P(("dp", "col"), "row"),
        P(("dp", "row"), "col"),
        P(("row", "dp"), "col"),
        P(("row", "dp")),
        P("col"),
    )
    sizes = (mesh.shape["dp"], mesh.shape["row"], mesh.shape["col"])
    return jax.shard_map(
        functools.partial(body, sizes),
        mesh=mesh,
        in_specs=placed,
        out_specs=(P(("row", "dp"), "col"), P(("row", "dp"), "col"), P(("row", "dp")), P("col")),
        check_vma=False,
    )
```

time: 2960 us -> 769 us (0.26)
  waiting for transfers between devices: 2680 us -> 237 us
  Pallas kernels: 0 us -> 204 us
  starting transfers between devices: 0.11 us -> 186 us
  local copies, waits for them, and re-layouts: 0.01 us -> 116 us
  blocking collectives: 103 us -> 0 us
  matrix products: 90.9 us -> 0 us
  other arithmetic: 77.8 us -> 9.46 us
    reduce_scatter x1 -> x0, waiting for transfers between devices: 2450 us -> none  [body(): lax.psum_scatter(token_product(act_rows, cot_rows), 'dp', scatter_dimensi...]
    ppermute x0 -> x164, waiting for transfers between devices: none -> 237 us  [the longest x63 213 us: shifted(): lax.ppermute(value, axis, [(i, (i + by) % size) for i in range(size)])]
    all_gather x2 -> x0, waiting for transfers between devices: 229 us -> none  [the longest x1 122 us: body(): act_rows = lax.all_gather(activations, 'col', axis=0, tiled=True)]
    pallas_call x0 -> x9, Pallas kernels: none -> 204 us  [the longest x8 135 us: product(): pl.pallas_call(functools.partial(product_kernel, len(blocks)), grid=(widt...]
    ppermute x0 -> x164, starting transfers between devices: none -> 186 us  [the longest x63 140 us: shifted(): lax.ppermute(value, axis, [(i, (i + by) % size) for i in range(size)])]
    psum x3 -> x0, blocking collectives: 103 us -> none  [the longest x1 61 us: body(): col_sum = lax.psum(jnp.sum(squared, axis=0), ('dp', 'row'))]
    dot_general x1 -> x0, matrix products: 90.9 us -> none  [token_product(): lax.dot_general(left, right, (((0,), (0,)), ((), ())), preferred_element_...]
    unnamed x4 -> x240, local copies, waits for them, and re-layouts: 0.01 us -> 48.4 us
  transfers between devices with their start and end apart: 3 -> 164, of which waited for: 3 -> 40; matrix products, arithmetic and copies ran while one was open for 0% -> 12% of each run, Pallas kernels for 0% -> 18%
where the time goes in v1:
time: 769 us; the launch traced here: 757 us
  waiting for transfers between devices  237 us (31%)
  Pallas kernels  204 us (27%)
  starting transfers between devices  186 us (24%)
  local copies, waits for them, and re-layouts  116 us (15%)
  other arithmetic  9.46 us (1%)
    ppermute x63, waiting for transfers between devices, shifted(): lax.ppermute(value, axis, [(i, (i + by) % size) for i in range(size)])  213 us
    ppermute x63, starting transfers between devices, shifted(): lax.ppermute(value, axis, [(i, (i + by) % size) for i in range(size)])  140 us
    pallas_call x8, Pallas kernels, product(): pl.pallas_call(functools.partial(product_kernel, len(blocks)), grid=(widt...  135 us
    pallas_call x1, Pallas kernels, weight_step(): pl.pallas_call(functools.partial(step_kernel, count, relative), grid=(cou...  69.1 us
    unnamed x240, local copies, waits for them, and re-layouts  48.4 us
    ppermute x101, starting transfers between devices, flipped(): return lax.ppermute(value, axis, [(i, i ^ bit) for i in range(size)])  46 us
    dynamic_slice x19, local copies, waits for them, and re-layouts, body(): act.append(lax.dynamic_index_in_dim(parts, at, 0, keepdims=False))  43.8 us
    ppermute x101, waiting for transfers between devices, flipped(): return lax.ppermute(value, axis, [(i, i ^ bit) for i in range(size)])  24.1 us
  transfers between devices with their start and end apart: 164, of which 40 were waited for; matrix products, arithmetic and copies ran while one was open for 12% of the time, Pallas kernels for 18%

profile of v1, /device:TPU:0, one launch (start us, length us, event | category | flops | bytes accessed | tf_op | source)
XLA Modules:
  0.0 757.2 jit_solution(13754017626878991699)
XLA Ops:
  11.5 10.4 %collective-permute-done.100.refs_4_ = bf16[256,1024]{1,0:T(8,128)(2,1)S(1)} collective-permute-done((bf16[256,1024]{1,0:T(8,128)(2,1)S(1)}, bf16[256,1024]{1,0:T(8,128)(2,1)S(1)}, u32[]{:S(2)}, u32[]{:S(2)}) %collective-permute-start.100) | collective-permute-done | bytes 524320 | tf_op jit(solution)/shard_map/ppermute | solution.py:114
  25.8 7.3 collective-permute-done.85.refs_4_
  48.3 7.3 collective-permute-done.55.refs_4_
  68.6 9.5 %collective-permute-done.25.refs_4_ = bf16[256,1024]{1,0:T(8,128)(2,1)} collective-permute-done((bf16[256,1024]{1,0:T(8,128)(2,1)S(1)}, bf16[256,1024]{1,0:T(8,128)(2,1)}, u32[]{:S(2)}, u32[]{:S(2)}) %collective-permute-start.25) | collective-permute-done | bytes 524320 | tf_op jit(solution)/shard_map/ppermute | solution.py:114
  82.6 32.1 %collective-permute-done.10.refs_4_ = bf16[256,1024]{1,0:T(8,128)(2,1)S(1)} collective-permute-done((bf16[256,1024]{1,0:T(8,128)(2,1)S(1)}, bf16[256,1024]{1,0:T(8,128)(2,1)S(1)}, u32[]{:S(2)}, u32[]{:S(2)}) %collective-permute-start.10) | collective-permute-done | bytes 524320 | tf_op jit(solution)/shard_map/ppermute | solution.py:114
  117.9 24.7 %collective-permute-start.3 = (bf16[512,1152]{1,0:T(8,128)(2,1)}, bf16[512,1152]{1,0:T(8,128)(2,1)}, u32[]{:S(2)}, u32[]{:S(2)}) collective-permute-start(bf16[512,1152]{1,0:T(8,128)(2,1)} %get-tuple-element.80), channel_id=1, source_target_pairs={{0,16},{8,24},{16,0},{24,8},{1,17},{9,25},{17,1},{25,9},{2,18},{10... | collective-permute-start | bytes 3538952 | tf_op jit(solution)/shard_map/ppermute | solution.py:114
  154.6 24.2 %collective-permute-start.104 = (bf16[256,1024]{1,0:T(8,128)(2,1)}, bf16[256,1024]{1,0:T(8,128)(2,1)S(1)}, u32[]{:S(2)}, u32[]{:S(2)}) collective-permute-start(bf16[256,1024]{1,0:T(8,128)(2,1)} %copy-done.26), channel_id=1, source_target_pairs={{0,8},{8,16},{16,24},{24,0},{1,9},{9,17},{17,25},{25,1},{2,10},{10... | collective-permute-start | bytes 1572872 | tf_op jit(solution)/shard_map/ppermute | solution.py:114
  182.8 7.9 %collective-permute-done.104.refs_8_ = bf16[256,1024]{1,0:T(8,128)(2,1)S(1)} collective-permute-done((bf16[256,1024]{1,0:T(8,128)(2,1)}, bf16[256,1024]{1,0:T(8,128)(2,1)S(1)}, u32[]{:S(2)}, u32[]{:S(2)}) %collective-permute-start.104) | collective-permute-done | bytes 524320 | tf_op jit(solution)/shard_map/ppermute | solution.py:114
  195.0 19.4 %collective-permute-start.89 = (bf16[256,1024]{1,0:T(8,128)(2,1)S(1)}, bf16[256,1024]{1,0:T(8,128)(2,1)S(1)}, u32[]{:S(2)}, u32[]{:S(2)}) collective-permute-start(bf16[256,1024]{1,0:T(8,128)(2,1)S(1)} %copy-done.19), channel_id=1, source_target_pairs={{0,8},{8,16},{16,24},{24,0},{1,9},{9,17},{17,25},{25,1},{2,10},{10... | collective-permute-start | bytes 1572872 | tf_op jit(solution)/shard_map/ppermute | solution.py:114
  218.1 11.1 %collective-permute-done.89.refs_8_ = bf16[256,1024]{1,0:T(8,128)(2,1)S(1)} collective-permute-done((bf16[256,1024]{1,0:T(8,128)(2,1)S(1)}, bf16[256,1024]{1,0:T(8,128)(2,1)S(1)}, u32[]{:S(2)}, u32[]{:S(2)}) %collective-permute-start.89) | collective-permute-done | bytes 524320 | tf_op jit(solution)/shard_map/ppermute | solution.py:114
  250.7 7.8 %collective-permute-done.6 = bf16[512,1152]{1,0:T(8,128)(2,1)} collective-permute-done((bf16[512,1152]{1,0:T(8,128)(2,1)}, bf16[512,1152]{1,0:T(8,128)(2,1)}, u32[]{:S(2)}, u32[]{:S(2)}) %collective-permute-start.6) | collective-permute-done | bytes 1179680 | tf_op jit(solution)/shard_map/ppermute | solution.py:114
  258.4 24.8 %collective-permute-done.4 = bf16[512,1152]{1,0:T(8,128)(2,1)} collective-permute-done((bf16[512,1152]{1,0:T(8,128)(2,1)}, bf16[512,1152]{1,0:T(8,128)(2,1)}, u32[]{:S(2)}, u32[]{:S(2)}) %collective-permute-start.4) | collective-permute-done | bytes 1179680 | tf_op jit(solution)/shard_map/ppermute | solution.py:114
  312.6 8.7 %collective-permute-done.29.refs_8_ = bf16[256,1024]{1,0:T(8,128)(2,1)} collective-permute-done((bf16[256,1024]{1,0:T(8,128)(2,1)}, bf16[256,1024]{1,0:T(8,128)(2,1)}, u32[]{:S(2)}, u32[]{:S(2)}) %collective-permute-start.29) | collective-permute-done | bytes 524320 | tf_op jit(solution)/shard_map/ppermute | solution.py:114
  354.0 7.9 %collective-permute-done.108.refs_12_ = bf16[256,1024]{1,0:T(8,128)(2,1)} collective-permute-done((bf16[256,1024]{1,0:T(8,128)(2,1)}, bf16[256,1024]{1,0:T(8,128)(2,1)}, u32[]{:S(2)}, u32[]{:S(2)}) %collective-permute-start.108) | collective-permute-done | bytes 524320 | tf_op jit(solution)/shard_map/ppermute | solution.py:114
  376.0 8.4 %collective-permute-done.78.refs_12_ = bf16[256,1024]{1,0:T(8,128)(2,1)} collective-permute-done((bf16[256,1024]{1,0:T(8,128)(2,1)}, bf16[256,1024]{1,0:T(8,128)(2,1)}, u32[]{:S(2)}, u32[]{:S(2)}) %collective-permute-start.78) | collective-permute-done | bytes 524320 | tf_op jit(solution)/shard_map/ppermute | solution.py:114
  449.0 16.9 %product.15 = (f32[1152,1024]{1,0:T(8,128)}, f32[1152,128]{1,0:T(8,128)}, f32[1,1024]{1,0:T(1,128)S(1)}) custom-call(bf16[1152,4096]{1,0:T(8,128)(2,1)} %bitcast.109, bf16[256,1024]{1,0:T(8,128)(2,1)} %get-tuple-element.88.refs_0_, bf16[256,1024]{1,0:T(8,128)(2,1)S(1)} %copy-done.53, bf16[256,1024]{1,0:T(8,128)(2,1)} %collective-permute-done.113.refs_2_, ...), custom_call_target="tpu_custom_call" | custom-call | flops 9663676416 | bytes 22544384 | tf_op jit(solution)/shard_map/product/pallas_call | solution.py:40
  468.7 16.8 %product.14 = (f32[1152,1024]{1,0:T(8,128)}, f32[1152,128]{1,0:T(8,128)}, f32[1,1024]{1,0:T(1,128)S(1)}) custom-call(bf16[1152,4096]{1,0:T(8,128)(2,1)} %bitcast.110, bf16[256,1024]{1,0:T(8,128)(2,1)S(1)} %copy-done.1, bf16[256,1024]{1,0:T(8,128)(2,1)S(1)} %copy-done.33, bf16[256,1024]{1,0:T(8,128)(2,1)S(1)} %copy-done.31, bf16[256,1024]{1,0:T(8,128)(2,1)S(1)} %copy-done.57, ...), custom_call_target="tpu_custom_call" | custom-call | flops 9663676416 | bytes 22544384 | tf_op jit(solution)/shard_map/product/pallas_call | solution.py:40
  493.2 16.9 %product.13 = (f32[1152,1024]{1,0:T(8,128)}, f32[1152,128]{1,0:T(8,128)}, f32[1,1024]{1,0:T(1,128)S(1)}) custom-call(bf16[1152,4096]{1,0:T(8,128)(2,1)} %bitcast.111, bf16[256,1024]{1,0:T(8,128)(2,1)S(1)} %get-tuple-element.82.refs_0_, bf16[256,1024]{1,0:T(8,128)(2,1)S(1)} %copy-done.25, bf16[256,1024]{1,0:T(8,128)(2,1)S(1)} %copy-done.23, ...), custom_call_target="tpu_custom_call" | custom-call | flops 9663676416 | bytes 22544384 | tf_op jit(solution)/shard_map/product/pallas_call | solution.py:40
  512.8 16.8 %product.12 = (f32[1152,1024]{1,0:T(8,128)}, f32[1152,128]{1,0:T(8,128)}, f32[1,1024]{1,0:T(1,128)S(1)}) custom-call(bf16[1152,4096]{1,0:T(8,128)(2,1)} %bitcast.112, bf16[256,1024]{1,0:T(8,128)(2,1)S(1)} %get-tuple-element.83.refs_0_, bf16[256,1024]{1,0:T(8,128)(2,1)S(1)} %copy-done.17, bf16[256,1024]{1,0:T(8,128)(2,1)S(1)} %copy-done.13, ...), custom_call_target="tpu_custom_call" | custom-call | flops 9663676416 | bytes 22544384 | tf_op jit(solution)/shard_map/product/pallas_call | solution.py:40
  538.4 16.8 %product.11 = (f32[1152,1024]{1,0:T(8,128)}, f32[1152,128]{1,0:T(8,128)}, f32[1,1024]{1,0:T(1,128)S(1)}) custom-call(bf16[1152,4096]{1,0:T(8,128)(2,1)} %bitcast.113, bf16[256,1024]{1,0:T(8,128)(2,1)S(1)} %get-tuple-element.84.refs_0_, bf16[256,1024]{1,0:T(8,128)(2,1)} %collective-permute-done.52.refs_1_, bf16[256,1024]{1,0:T(8,128)(2,1)S(1)} %copy-done.9, ...), custom_call_target="tpu_custom_call" | custom-call | flops 9663676416 | bytes 22544384 | tf_op jit(solution)/shard_map/product/pallas_call | solution.py:40
  557.4 16.7 %product.10 = (f32[1152,1024]{1,0:T(8,128)}, f32[1152,128]{1,0:T(8,128)}, f32[1,1024]{1,0:T(1,128)S(1)}) custom-call(bf16[1152,4096]{1,0:T(8,128)(2,1)} %bitcast.114, bf16[256,1024]{1,0:T(8,128)(2,1)S(1)} %get-tuple-element.85.refs_0_, bf16[256,1024]{1,0:T(8,128)(2,1)} %collective-permute-done.37.refs_1_, bf16[256,1024]{1,0:T(8,128)(2,1)} %collective-permute-done.38.refs_2_, ...), custom_call_target="tpu_custom_call" | custom-call | flops 9663676416 | bytes 22544384 | tf_op jit(solution)/shard_map/product/pallas_call | solution.py:40
  576.2 16.8 %product.8 = (f32[1152,1024]{1,0:T(8,128)}, f32[1152,128]{1,0:T(8,128)}, f32[1,1024]{1,0:T(1,128)S(1)}) custom-call(bf16[1152,4096]{1,0:T(8,128)(2,1)} %bitcast.115, bf16[256,1024]{1,0:T(8,128)(2,1)S(1)} %get-tuple-element.87.refs_0_, bf16[256,1024]{1,0:T(8,128)(2,1)} %collective-permute-done.7.refs_1_, bf16[256,1024]{1,0:T(8,128)(2,1)S(1)} %copy-done.15, ...), custom_call_target="tpu_custom_call" | custom-call | flops 9663676416 | bytes 22544384 | tf_op jit(solution)/shard_map/product/pallas_call | solution.py:40
  595.4 17.0 %product.9 = (f32[1152,1024]{1,0:T(8,128)}, f32[1152,128]{1,0:T(8,128)}, f32[1,1024]{1,0:T(1,128)S(1)}) custom-call(bf16[1152,4096]{1,0:T(8,128)(2,1)} %bitcast.116, bf16[256,1024]{1,0:T(8,128)(2,1)S(1)} %get-tuple-element.86.refs_0_, bf16[256,1024]{1,0:T(8,128)(2,1)S(1)} %copy-done.5, bf16[256,1024]{1,0:T(8,128)(2,1)S(1)} %copy-done.3, ...), custom_call_target="tpu_custom_call" | custom-call | flops 9663676416 | bytes 22544384 | tf_op jit(solution)/shard_map/product/pallas_call | solution.py:40
  687.8 69.1 %weight_step.1 = (f32[1152,8192]{1,0:T(8,128)}, bf16[1152,8192]{1,0:T(8,128)(2,1)}) custom-call(f32[1,1]{1,0:T(1,128)S(6)} %div.90.clip_ref, f32[1152,1]{1,0:T(8,128)S(1)} %broadcast_in_dim.46.row_ref, f32[1,8192]{1,0:T(1,128)S(1)} %rsqrt.14.col_ref, f32[1152,8192]{1,0:T(8,128)} %weight_ref.1, f32[1152,1024]{1,0:T(8,128)S(1)} %bitcast.71, ...), custom_call_target="tpu_custom_call" | custom-call | flops 47185920 | bytes 132120576 | tf_op jit(solution)/shard_map/weight_step/pallas_call | solution.py:87
  (652 shorter events, 336.4 us)
Async XLA Ops:
  66.9 87.7 %collective-permute-start.1 = (bf16[512,1152]{1,0:T(8,128)(2,1)}, bf16[512,1152]{1,0:T(8,128)(2,1)}, u32[]{:S(2)}, u32[]{:S(2)}) collective-permute-start(bf16[512,1152]{1,0:T(8,128)(2,1)} %get-tuple-element.79), channel_id=1, source_target_pairs={{0,8},{8,16},{16,24},{24,0},{1,9},{9,17},{17,25},{25,1},{2,10},{10... | collective-permute-start | bytes 3538952 | tf_op jit(solution)/shard_map/ppermute | solution.py:114
  67.0 47.6 %collective-permute-start.10 = (bf16[256,1024]{1,0:T(8,128)(2,1)S(1)}, bf16[256,1024]{1,0:T(8,128)(2,1)S(1)}, u32[]{:S(2)}, u32[]{:S(2)}) collective-permute-start(bf16[256,1024]{1,0:T(8,128)(2,1)S(1)} %get-tuple-element.87.refs_0_), channel_id=1, source_target_pairs={{0,8},{8,16},{16,24},{24,0},{1,9},{9,17},{17,25},{25,1},{2,10},{10... | collective-permute-start | bytes 1572872 | tf_op jit(solution)/shard_map/ppermute | solution.py:114
  78.2 36.5 %collective-permute-start.8 = (bf16[256,1024]{1,0:T(8,128)(2,1)S(1)}, bf16[256,1024]{1,0:T(8,128)(2,1)S(1)}, u32[]{:S(2)}, u32[]{:S(2)}) collective-permute-start(bf16[256,1024]{1,0:T(8,128)(2,1)S(1)} %get-tuple-element.87.refs_0_), channel_id=1, source_target_pairs={{0,4},{2,6},{4,0},{6,2},{1,5},{3,7},{5,1},{7,3},{8,12},{10,14},{12... | collective-permute-start | bytes 1572872 | tf_op jit(solution)/shard_map/ppermute | solution.py:114
  79.9 38.0 %collective-permute-start.7 = (bf16[256,1024]{1,0:T(8,128)(2,1)S(1)}, bf16[256,1024]{1,0:T(8,128)(2,1)}, u32[]{:S(2)}, u32[]{:S(2)}) collective-permute-start(bf16[256,1024]{1,0:T(8,128)(2,1)S(1)} %get-tuple-element.87.refs_0_), channel_id=1, source_target_pairs={{0,2},{2,0},{4,6},{6,4},{1,3},{3,1},{5,7},{7,5},{8,10},{10,8},{12,... | collective-permute-start | bytes 1572872 | tf_op jit(solution)/shard_map/ppermute | solution.py:118
  80.8 109.9 %collective-permute-start.5 = (bf16[512,1152]{1,0:T(8,128)(2,1)}, bf16[512,1152]{1,0:T(8,128)(2,1)}, u32[]{:S(2)}, u32[]{:S(2)}) collective-permute-start(bf16[512,1152]{1,0:T(8,128)(2,1)} %get-tuple-element.78), channel_id=1, source_target_pairs={{0,24},{8,0},{16,8},{24,16},{1,25},{9,1},{17,9},{25,17},{2,26},{10... | collective-permute-start | bytes 3538952 | tf_op jit(solution)/shard_map/ppermute | solution.py:114
  114.6 38.4 %collective-permute-start.115 = (bf16[256,1024]{1,0:T(8,128)(2,1)}, bf16[256,1024]{1,0:T(8,128)(2,1)}, u32[]{:S(2)}, u32[]{:S(2)}) collective-permute-start(bf16[256,1024]{1,0:T(8,128)(2,1)} %get-tuple-element.88.refs_0_), channel_id=1, source_target_pairs={{0,8},{8,16},{16,24},{24,0},{1,9},{9,17},{17,25},{25,1},{2,10},{10... | collective-permute-start | bytes 1572872 | tf_op jit(solution)/shard_map/ppermute | solution.py:114
  116.2 36.8 %collective-permute-start.113 = (bf16[256,1024]{1,0:T(8,128)(2,1)}, bf16[256,1024]{1,0:T(8,128)(2,1)}, u32[]{:S(2)}, u32[]{:S(2)}) collective-permute-start(bf16[256,1024]{1,0:T(8,128)(2,1)} %get-tuple-element.88.refs_0_), channel_id=1, source_target_pairs={{0,4},{2,6},{4,0},{6,2},{1,5},{3,7},{5,1},{7,3},{8,12},{10,14},{12... | collective-permute-start | bytes 1572872 | tf_op jit(solution)/shard_map/ppermute | solution.py:114
  117.9 97.9 %collective-permute-start.3 = (bf16[512,1152]{1,0:T(8,128)(2,1)}, bf16[512,1152]{1,0:T(8,128)(2,1)}, u32[]{:S(2)}, u32[]{:S(2)}) collective-permute-start(bf16[512,1152]{1,0:T(8,128)(2,1)} %get-tuple-element.80), channel_id=1, source_target_pairs={{0,16},{8,24},{16,0},{24,8},{1,17},{9,25},{17,1},{25,9},{2,18},{10... | collective-permute-start | bytes 3538952 | tf_op jit(solution)/shard_map/ppermute | solution.py:114
  153.0 27.4 %collective-permute-start.112 = (bf16[256,1024]{1,0:T(8,128)(2,1)}, bf16[256,1024]{1,0:T(8,128)(2,1)S(1)}, u32[]{:S(2)}, u32[]{:S(2)}) collective-permute-start(bf16[256,1024]{1,0:T(8,128)(2,1)} %get-tuple-element.88.refs_0_), channel_id=1, source_target_pairs={{0,2},{2,0},{4,6},{6,4},{1,3},{3,1},{5,7},{7,5},{8,10},{10,8},{12,... | collective-permute-start | bytes 1572872 | tf_op jit(solution)/shard_map/ppermute | solution.py:118
  153.0 76.8 %collective-permute-start = (bf16[512,1152]{1,0:T(8,128)(2,1)}, bf16[512,1152]{1,0:T(8,128)(2,1)S(1)}, u32[]{:S(2)}, u32[]{:S(2)}) collective-permute-start(bf16[512,1152]{1,0:T(8,128)(2,1)} %get-tuple-element.77), channel_id=1, source_target_pairs={{0,1},{1,0},{2,3},{3,2},{4,5},{5,4},{6,7},{7,6},{8,9},{9,8},{10,11... | collective-permute-start | bytes 3538952 | tf_op jit(solution)/shard_map/ppermute | solution.py:114
  154.6 36.0 %collective-permute-start.104 = (bf16[256,1024]{1,0:T(8,128)(2,1)}, bf16[256,1024]{1,0:T(8,128)(2,1)S(1)}, u32[]{:S(2)}, u32[]{:S(2)}) collective-permute-start(bf16[256,1024]{1,0:T(8,128)(2,1)} %copy-done.26), channel_id=1, source_target_pairs={{0,8},{8,16},{16,24},{24,0},{1,9},{9,17},{17,25},{25,1},{2,10},{10... | collective-permute-start | bytes 1572872 | tf_op jit(solution)/shard_map/ppermute | solution.py:114
  190.6 45.3 %collective-permute-start.2 = (bf16[512,1152]{1,0:T(8,128)(2,1)}, bf16[512,1152]{1,0:T(8,128)(2,1)S(1)}, u32[]{:S(2)}, u32[]{:S(2)}) collective-permute-start(bf16[512,1152]{1,0:T(8,128)(2,1)} %collective-permute-done.1), channel_id=1, source_target_pairs={{0,1},{1,0},{2,3},{3,2},{4,5},{5,4},{6,7},{7,6},{8,9},{9,8},{10,11... | collective-permute-start | bytes 3538952 | tf_op jit(solution)/shard_map/ppermute | solution.py:114
  195.0 34.3 %collective-permute-start.89 = (bf16[256,1024]{1,0:T(8,128)(2,1)S(1)}, bf16[256,1024]{1,0:T(8,128)(2,1)S(1)}, u32[]{:S(2)}, u32[]{:S(2)}) collective-permute-start(bf16[256,1024]{1,0:T(8,128)(2,1)S(1)} %copy-done.19), channel_id=1, source_target_pairs={{0,8},{8,16},{16,24},{24,0},{1,9},{9,17},{17,25},{25,1},{2,10},{10... | collective-permute-start | bytes 1572872 | tf_op jit(solution)/shard_map/ppermute | solution.py:114
  229.3 29.2 %collective-permute-start.6 = (bf16[512,1152]{1,0:T(8,128)(2,1)}, bf16[512,1152]{1,0:T(8,128)(2,1)}, u32[]{:S(2)}, u32[]{:S(2)}) collective-permute-start(bf16[512,1152]{1,0:T(8,128)(2,1)} %collective-permute-done.5), channel_id=1, source_target_pairs={{0,1},{1,0},{2,3},{3,2},{4,5},{5,4},{6,7},{7,6},{8,9},{9,8},{10,11... | collective-permute-start | bytes 3538952 | tf_op jit(solution)/shard_map/ppermute | solution.py:114
  229.9 53.4 %collective-permute-start.4 = (bf16[512,1152]{1,0:T(8,128)(2,1)}, bf16[512,1152]{1,0:T(8,128)(2,1)}, u32[]{:S(2)}, u32[]{:S(2)}) collective-permute-start(bf16[512,1152]{1,0:T(8,128)(2,1)} %collective-permute-done.3), channel_id=1, source_target_pairs={{0,1},{1,0},{2,3},{3,2},{4,5},{5,4},{6,7},{7,6},{8,9},{9,8},{10,11... | collective-permute-start | bytes 3538952 | tf_op jit(solution)/shard_map/ppermute | solution.py:114
  249.1 45.2 %collective-permute-start.59 = (bf16[256,1024]{1,0:T(8,128)(2,1)}, bf16[256,1024]{1,0:T(8,128)(2,1)}, u32[]{:S(2)}, u32[]{:S(2)}) collective-permute-start(bf16[256,1024]{1,0:T(8,128)(2,1)} %copy-done.6), channel_id=1, source_target_pairs={{0,8},{8,16},{16,24},{24,0},{1,9},{9,17},{17,25},{25,1},{2,10},{10... | collective-permute-start | bytes 1572872 | tf_op jit(solution)/shard_map/ppermute | solution.py:114
  249.2 46.6 %collective-permute-start.57 = (bf16[256,1024]{1,0:T(8,128)(2,1)}, bf16[256,1024]{1,0:T(8,128)(2,1)}, u32[]{:S(2)}, u32[]{:S(2)}) collective-permute-start(bf16[256,1024]{1,0:T(8,128)(2,1)} %copy-done.6), channel_id=1, source_target_pairs={{0,4},{2,6},{4,0},{6,2},{1,5},{3,7},{5,1},{7,3},{8,12},{10,14},{12... | collective-permute-start | bytes 1572872 | tf_op jit(solution)/shard_map/ppermute | solution.py:114
  250.7 45.2 %collective-permute-start.56 = (bf16[256,1024]{1,0:T(8,128)(2,1)}, bf16[256,1024]{1,0:T(8,128)(2,1)S(1)}, u32[]{:S(2)}, u32[]{:S(2)}) collective-permute-start(bf16[256,1024]{1,0:T(8,128)(2,1)} %copy-done.6), channel_id=1, source_target_pairs={{0,2},{2,0},{4,6},{6,4},{1,3},{3,1},{5,7},{7,5},{8,10},{10,8},{12,... | collective-permute-start | bytes 1572872 | tf_op jit(solution)/shard_map/ppermute | solution.py:118
  258.4 28.0 %collective-permute-start.69 = (bf16[256,1024]{1,0:T(8,128)(2,1)}, bf16[256,1024]{1,0:T(8,128)(2,1)S(1)}, u32[]{:S(2)}, u32[]{:S(2)}) collective-permute-start(bf16[256,1024]{1,0:T(8,128)(2,1)} %copy-done.12), channel_id=1, source_target_pairs={{0,2},{2,0},{4,6},{6,4},{1,3},{3,1},{5,7},{7,5},{8,10},{10,8},{12,... | collective-permute-start | bytes 1572872 | tf_op jit(solution)/shard_map/ppermute | solution.py:118
  486.5 25.2 %collective-permute-start.79 = (bf16[256,1024]{1,0:T(8,128)(2,1)}, bf16[256,1024]{1,0:T(8,128)(2,1)S(1)}, u32[]{:S(2)}, u32[]{:S(2)}) collective-permute-start(bf16[256,1024]{1,0:T(8,128)(2,1)} %collective-permute-done.78.refs_12_), channel_id=1, source_target_pairs={{0,2},{2,0},{4,6},{6,4},{1,3},{3,1},{5,7},{7,5},{8,10},{10,8},{12,... | collective-permute-start | bytes 1572872 | tf_op jit(solution)/shard_map/ppermute | solution.py:118
  486.7 25.2 %collective-permute-start.77 = (bf16[256,1024]{1,0:T(8,128)(2,1)}, bf16[256,1024]{1,0:T(8,128)(2,1)S(1)}, u32[]{:S(2)}, u32[]{:S(2)}) collective-permute-start(bf16[256,1024]{1,0:T(8,128)(2,1)} %collective-permute-done.76.refs_10_), channel_id=1, source_target_pairs={{0,2},{2,0},{4,6},{6,4},{1,3},{3,1},{5,7},{7,5},{8,10},{10,8},{12,... | collective-permute-start | bytes 1572872 | tf_op jit(solution)/shard_map/ppermute | solution.py:118
  529.7 25.5 %collective-permute-start.15 = (bf16[256,1024]{1,0:T(8,128)(2,1)}, bf16[256,1024]{1,0:T(8,128)(2,1)S(1)}, u32[]{:S(2)}, u32[]{:S(2)}) collective-permute-start(bf16[256,1024]{1,0:T(8,128)(2,1)} %collective-permute-done.14.refs_8_), channel_id=1, source_target_pairs={{0,2},{2,0},{4,6},{6,4},{1,3},{3,1},{5,7},{7,5},{8,10},{10,8},{12,... | collective-permute-start | bytes 1572872 | tf_op jit(solution)/shard_map/ppermute | solution.py:118
  530.2 25.5 %collective-permute-start.49 = (bf16[256,1024]{1,0:T(8,128)(2,1)}, bf16[256,1024]{1,0:T(8,128)(2,1)S(1)}, u32[]{:S(2)}, u32[]{:S(2)}) collective-permute-start(bf16[256,1024]{1,0:T(8,128)(2,1)} %collective-permute-done.48.refs_12_), channel_id=1, source_target_pairs={{0,2},{2,0},{4,6},{6,4},{1,3},{3,1},{5,7},{7,5},{8,10},{10,8},{12,... | collective-permute-start | bytes 1572872 | tf_op jit(solution)/shard_map/ppermute | solution.py:118
  530.3 25.5 %collective-permute-start.47 = (bf16[256,1024]{1,0:T(8,128)(2,1)}, bf16[256,1024]{1,0:T(8,128)(2,1)S(1)}, u32[]{:S(2)}, u32[]{:S(2)}) collective-permute-start(bf16[256,1024]{1,0:T(8,128)(2,1)} %collective-permute-done.46.refs_10_), channel_id=1, source_target_pairs={{0,2},{2,0},{4,6},{6,4},{1,3},{3,1},{5,7},{7,5},{8,10},{10,8},{12,... | collective-permute-start | bytes 1572872 | tf_op jit(solution)/shard_map/ppermute | solution.py:118
  (249 other events, 4060.5 us)

commit v2 on v0

v2 whole, which is shorter than its diff:
```python
import functools

import jax
import jax.numpy as jnp
from jax import lax
from jax.experimental import pallas as pl
from jax.experimental.pallas import tpu as pltpu
from jax.sharding import PartitionSpec as P

D = 18432
F = 16384
STEP = 10
SHARES = (4, 4, 4, 4)
LAST_SHARES = (4, 4, 4, 2, 1, 1)


def product_kernel(count, adds, place_ref, act_ref, *refs):
    blocks, (grad_ref, col_ref, *row_ref, held) = refs[:count], refs[-4 if adds else -3 :]
    depth = blocks[0].shape[0]
    for k, block in enumerate(blocks):
        held[pl.ds(pl.multiple_of(place_ref[k] * depth, depth), depth), :] = block[...]
    grad = jnp.dot(act_ref[...], held[...], preferred_element_type=jnp.float32)
    if not adds:
        grad_ref[...] = grad
        col_ref[...] = grad[:1, :]
        return
    grad = grad + refs[count][...]
    grad_ref[...] = grad
    squared = grad * grad
    col_ref[...] = jnp.sum(squared, axis=0, keepdims=True)
    lanes = squared[:, :128]
    for at in range(128, squared.shape[1], 128):
        lanes = lanes + squared[:, at : at + 128]

    @pl.when(pl.program_id(0) == 0)
    def _():
        row_ref[0][...] = jnp.zeros_like(row_ref[0])

    row_ref[0][...] += lanes


def product(act, half, places, blocks, start, width, grad, columns):
    rows, tokens = act.shape[0], act.shape[1] // 2
    blocks, origins = zip(*blocks)
    depth = blocks[0].shape[0]
    tile = next(t for t in (512, 256, 128) if width % t == 0 and start % t == 0)
    first = start // tile
    adds = half == 1
    before = [] if grad is None else [grad]
    in_place = pl.BlockSpec((rows, tile), lambda j, _: (0, first + j))
    return pl.pallas_call(
        functools.partial(product_kernel, len(blocks), adds),
        grid_spec=pltpu.PrefetchScalarGridSpec(
            num_scalar_prefetch=1,
            grid=(width // tile,),
            in_specs=[pl.BlockSpec((rows, tokens), lambda j, _: (0, half))]
            + [
                pl.BlockSpec((depth, tile), lambda j, _, at=(start - origin) // tile: (0, at + j))
                for origin in origins
            ]
            + [in_place if adds else pl.BlockSpec(memory_space=pl.ANY)] * len(before),
            out_specs=[in_place, pl.BlockSpec((1, tile), lambda j, _: (0, j))]
            + ([pl.BlockSpec((rows, 128), lambda j, _: (0, 0))] if adds else []),
            scratch_shapes=[pltpu.VMEM((tokens, tile), jnp.bfloat16)],
        ),
        out_shape=[
            jax.ShapeDtypeStruct((rows, columns), jnp.float32),
            jax.ShapeDtypeStruct((1, width), jnp.float32),
        ]
        + ([jax.ShapeDtypeStruct((rows, 128), jnp.float32)] if adds else []),
        input_output_aliases={len(blocks) + 2: 0} if before else {},
        cost_estimate=pl.CostEstimate(
            flops=2 * rows * tokens * width,
            bytes_accessed=2 * (rows + width) * tokens + 4 * (2 if adds else 1) * rows * width,
            transcendentals=0,
        ),
        compiler_params=pltpu.CompilerParams(vmem_limit_bytes=44 * 2**20),
        name="product",
    )(places, act, *blocks, *before)


def step_kernel(relative, clip_ref, row_ref, col_ref, weight_ref, grad_ref, new_ref, clipped_ref):
    clipped = grad_ref[...] * (row_ref[...] * clip_ref[0, 0]) * col_ref[...]
    new_ref[...] = weight_ref[...] - relative * clipped
    clipped_ref[...] = clipped.astype(jnp.bfloat16)


def weight_step(relative, inverse_clip, row_scale, col_scale, weight, grad):
    rows, columns = weight.shape
    tile = next(t for t in (64, 32, 16) if rows % t == 0)
    block = pl.BlockSpec((tile, columns), lambda i: (i, 0))
    return pl.pallas_call(
        functools.partial(step_kernel, relative),
        grid=(rows // tile,),
        in_specs=[
            pl.BlockSpec(memory_space=pltpu.SMEM),
            pl.BlockSpec((tile, 1), lambda i: (i, 0)),
            pl.BlockSpec((1, columns), lambda i: (0, 0)),
            block,
            block,
        ],
        out_specs=[block, block],
        out_shape=[
            jax.ShapeDtypeStruct((rows, columns), jnp.float32),
            jax.ShapeDtypeStruct((rows, columns), jnp.bfloat16),
        ],
        cost_estimate=pl.CostEstimate(
            flops=5 * rows * columns, bytes_accessed=14 * rows * columns, transcendentals=0
        ),
        compiler_params=pltpu.CompilerParams(vmem_limit_bytes=40 * 2**20),
        name="weight_step",
    )(inverse_clip.reshape(1, 1), row_scale[:, None], col_scale[None, :], weight, grad)


class Lane:
    def __init__(self, axis, size, ahead):
        self.axis, self.size, self.ahead, self.sent = axis, size, ahead, []

    def send(self, value, target, after=()):
        value = lax.optimization_barrier((value, *after))[0] if after else value
        if len(self.sent) >= self.ahead:
            value, _ = lax.optimization_barrier((value, self.sent[-self.ahead]))
        value = lax.ppermute(value, self.axis, [(i, target(i)) for i in range(self.size)])
        self.sent.append(value)
        return value

    def shift(self, value, by, after=()):
        return self.send(value, lambda i: (i + by) % self.size, after)

    def flip(self, value, bit):
        return self.send(value, lambda i: i ^ bit)


def total(value, axis, size):
    if size & (size - 1):
        return lax.psum(value, axis)
    bit = 1
    while bit < size:
        value = value + lax.ppermute(value, axis, [(i, i ^ bit) for i in range(size)])
        bit *= 2
    return value


def body(sizes, activations, cotangent, weight, row_moment, col_moment):
    n_dp, n_row, n_col = sizes
    n_x = n_row // 2
    z, r, y = lax.axis_index("dp"), lax.axis_index("row"), lax.axis_index("col")
    decay_rate = 1.0 - float(STEP) ** (-0.8)
    relative = min(0.01, float(STEP) ** (-0.5))
    rows = weight.shape[0]
    columns = cotangent.shape[1]
    along_z, along_x, along_y, cores = Lane("dp", n_dp, 2), Lane("row", n_row, 2), Lane("col", n_col, 2), Lane("row", n_row, 4)

    def over_rows(value):
        return total(total(value, "row", n_row), "dp", n_dp)

    own = []
    for u in range(n_x):
        across = along_x.shift(cotangent, 2 * u) if u else cotangent
        own += [across, cores.flip(across, 1)]

    pieces = []
    for s in range(n_dp):
        to = lax.rem(z + s, n_dp)
        piece = lax.dynamic_slice_in_dim(activations, to * rows, rows, axis=1)
        pieces.append(along_z.shift(piece, s) if s else piece)
    act = []
    for piece in pieces:
        parts = [along_y.shift(piece, t) if t else piece for t in range(n_col)]
        ordered = [parts[0]] * n_col
        for at in range(n_col):
            for t in range(1, n_col):
                ordered[at] = jnp.where(lax.rem(y - t + n_col, n_col) == at, parts[t], ordered[at])
        act += ordered
    act = jnp.concatenate(act, axis=0).T
    half = n_dp // 2
    places = jnp.stack(
        [
            n_row * s + (lax.rem(r - 2 * u + n_row, n_row) ^ v)
            for s in range(half)
            for u in range(n_x)
            for v in range(2)
        ]
    ).astype(jnp.int32)

    def cut(shares):
        widths = [columns * share // sum(shares) for share in shares]
        return [(sum(widths[:k]), width) for k, width in enumerate(widths)]

    moving = [(start, cotangent[:, start : start + width]) for start, width in cut(SHARES)]
    first_half, second_half = [(block, 0) for block in own], []
    grad, row_lanes, weighted, col_new = None, 0.0, 0.0, []
    first_done, col_sums, lasts = [], [], cut(LAST_SHARES)
    starts = [start for start, _ in lasts]
    count = 0
    for s in range(1, n_dp):
        last = s == n_dp - 1
        if last:
            holders = [max(k for k, (start, _) in enumerate(moving) if start <= at) for at in starts]
            moving = [
                (at, moving[k][1][:, at - moving[k][0] : at - moving[k][0] + width])
                for k, (at, width) in zip(holders, lasts)
            ]
        for k, (start, block) in enumerate(moving):
            width = block.shape[1]
            after = ()
            if s >= half:
                after = (first_done[count - 2],) if 0 <= count - 2 < len(first_done) else (act,) if count == 0 else ()
                count += 1
            block = along_z.shift(block, 1, after)
            moving[k] = (start, block)
            arrived = []
            for u in range(n_x):
                after = (col_sums[k - 3],) if last and u and k >= 3 else ()
                across = along_x.shift(block, 2 * u, after) if u else block
                arrived += [(across, start), (cores.flip(across, 1), start)]
            if s < half:
                first_half_here = first_half + arrived
                grad, token = product(act, 0, places, first_half_here, start, width, grad, columns)
                first_done.append(token)
            elif not last:
                second_half.append((start, width, arrived))
            else:
                earlier = [b for at, size, blocks in second_half if at <= start < at + size for b in blocks]
                grad, col_part, row_part = product(act, 1, places, earlier + arrived, start, width, grad, columns)
                row_lanes = row_lanes + row_part
                col_sums.append(col_part)
            if last and (k == 1 or k == 3):
                low, high = starts[k - 1], start + width
                col_sum = jnp.concatenate(col_sums[k - 1 : k + 1], axis=1)
                col_new.append(
                    decay_rate * col_moment[low:high] + (1.0 - decay_rate) * over_rows(col_sum)[0] / D
                )
                squared = jnp.square(grad[:, low:high])
                weighted = weighted + jnp.sum(squared * (1.0 / col_new[-1])[None, :], axis=1)
                grad, weighted = lax.optimization_barrier((grad, weighted))
    low, high = starts[4], columns
    col_sum = jnp.concatenate(col_sums[4:], axis=1)
    squared = jnp.square(grad[:, low:high])
    held = decay_rate * col_moment[low:high]
    row_new = decay_rate * row_moment + (1.0 - decay_rate) * total(jnp.sum(row_lanes, axis=1), "col", n_col) / F
    by_row = jnp.full((1, 128), jnp.sum(weighted / row_new) / 128)
    by_col = jnp.sum(squared * (1.0 / row_new)[:, None], axis=0, keepdims=True)
    sums = over_rows(jnp.concatenate([col_sum, by_col, by_row], axis=1))[0]
    count = high - low
    col_new.append(held + (1.0 - decay_rate) * sums[:count] / D)
    update_total = jnp.sum(sums[count : 2 * count] / col_new[-1]) + jnp.sum(sums[2 * count :])
    update_total = total(update_total.reshape(1, 1), "col", n_col)[0, 0]
    col_new = jnp.concatenate(col_new)
    clip_factor = jnp.maximum(1.0, jnp.sqrt(update_total / (D * F)))
    new_weight, clipped = weight_step(
        relative, 1.0 / clip_factor, lax.rsqrt(row_new), lax.rsqrt(col_new), weight, grad
    )
    return (new_weight, clipped, row_new, col_new)


def solution(mesh):
    placed = (
        P(("dp", "col"), "row"),
        P(("dp", "row"), "col"),
        P(("row", "dp"), "col"),
        P(("row", "dp")),
        P("col"),
    )
    sizes = (mesh.shape["dp"], mesh.shape["row"], mesh.shape["col"])
    return jax.shard_map(
        functools.partial(body, sizes),
        mesh=mesh,
        in_specs=placed,
        out_specs=(P(("row", "dp"), "col"), P(("row", "dp"), "col"), P(("row", "dp")), P("col")),
        check_vma=False,
    )
```

time: 2960 us -> 692 us (0.23)
  waiting for transfers between devices: 2680 us -> 365 us
  Pallas kernels: 0 us -> 193 us
  blocking collectives: 103 us -> 0 us
  matrix products: 90.9 us -> 0 us
  starting transfers between devices: 0.11 us -> 52.5 us
  other arithmetic: 77.8 us -> 26.4 us
  local copies, waits for them, and re-layouts: 0.01 us -> 43.5 us
    reduce_scatter x1 -> x0, waiting for transfers between devices: 2450 us -> none  [body(): lax.psum_scatter(token_product(act_rows, cot_rows), 'dp', scatter_dimensi...]
    ppermute x0 -> x80, waiting for transfers between devices: none -> 365 us  [the longest x66 334 us: send(): lax.ppermute(value, self.axis, [(i, target(i)) for i in range(self.size)])]
    all_gather x2 -> x0, waiting for transfers between devices: 229 us -> none  [the longest x1 122 us: body(): act_rows = lax.all_gather(activations, 'col', axis=0, tiled=True)]
    pallas_call x0 -> x11, Pallas kernels: none -> 193 us  [the longest x10 146 us: product(): pl.pallas_call(functools.partial(product_kernel, len(blocks), adds), grid...]
    psum x3 -> x0, blocking collectives: 103 us -> none  [the longest x1 61 us: body(): col_sum = lax.psum(jnp.sum(squared, axis=0), ('dp', 'row'))]
    dot_general x1 -> x0, matrix products: 90.9 us -> none  [token_product(): lax.dot_general(left, right, (((0,), (0,)), ((), ())), preferred_element_...]
    ppermute x0 -> x80, starting transfers between devices: none -> 52.5 us  [the longest x66 37 us: send(): lax.ppermute(value, self.axis, [(i, target(i)) for i in range(self.size)])]
    convert_element_type x1 -> x0, other arithmetic: 44.5 us -> none  [body(): return (new_weight, clipped.astype(jnp.bfloat16), row_new, col_new)]
  transfers between devices with their start and end apart: 3 -> 80, of which waited for: 3 -> 29; matrix products, arithmetic and copies ran while one was open for 0% -> 4% of each run, Pallas kernels for 0% -> 20%
where the time goes in v2:
time: 692 us; the launch traced here: 685 us
  waiting for transfers between devices  365 us (53%)
  Pallas kernels  193 us (28%)
  starting transfers between devices  52.5 us (8%)
  local copies, waits for them, and re-layouts  43.5 us (6%)
  other arithmetic  26.4 us (4%)
    ppermute x66, waiting for transfers between devices, send(): lax.ppermute(value, self.axis, [(i, target(i)) for i in range(self.size)])  334 us
    pallas_call x10, Pallas kernels, product(): pl.pallas_call(functools.partial(product_kernel, len(blocks), adds), grid...  146 us
    pallas_call x1, Pallas kernels, weight_step(): pl.pallas_call(functools.partial(step_kernel, relative), grid=(rows // ti...  47.2 us
    ppermute x66, starting transfers between devices, send(): lax.ppermute(value, self.axis, [(i, target(i)) for i in range(self.size)])  37 us
    unnamed x127, local copies, waits for them, and re-layouts  34.1 us
    ppermute x14, waiting for transfers between devices, total(): lax.ppermute(value, axis, [(i, i ^ bit) for i in range(size)])  30.9 us
    ppermute x14, starting transfers between devices, total(): lax.ppermute(value, axis, [(i, i ^ bit) for i in range(size)])  15.5 us
    reduce_sum x2, other arithmetic, body(): jnp.sum(squared * (1.0 / col_new[-1])[None, :], axis=1)  14.9 us
  transfers between devices with their start and end apart: 80, of which 29 were waited for; matrix products, arithmetic and copies ran while one was open for 4% of the time, Pallas kernels for 20%

profile of v2, /device:TPU:0, one launch (start us, length us, event | category | flops | bytes accessed | tf_op | source)
XLA Modules:
  0.0 685.1 jit_solution(14599355101486869711)
XLA Ops:
  22.9 12.6 %collective-permute-done = bf16[512,1152]{0,1:T(8,128)(2,1)} collective-permute-done((bf16[512,1152]{0,1:T(8,128)(2,1)S(1)}, bf16[512,1152]{0,1:T(8,128)(2,1)}, u32[]{:S(2)}, u32[]{:S(2)}) %collective-permute-start) | collective-permute-done | bytes 1179680 | tf_op jit(solution)/shard_map/ppermute | solution.py:123
  35.5 55.5 %collective-permute-done.3 = bf16[512,1152]{0,1:T(8,128)(2,1)} collective-permute-done((bf16[512,1152]{0,1:T(8,128)(2,1)}, bf16[512,1152]{0,1:T(8,128)(2,1)}, u32[]{:S(2)}, u32[]{:S(2)}) %collective-permute-start.3) | collective-permute-done | bytes 1179680 | tf_op jit(solution)/shard_map/ppermute | solution.py:123
  95.4 48.0 %collective-permute-done.26.refs_4_ = bf16[256,2048]{1,0:T(8,128)(2,1)S(1)} collective-permute-done((bf16[256,2048]{1,0:T(8,128)(2,1)S(1)}, bf16[256,2048]{1,0:T(8,128)(2,1)S(1)}, u32[]{:S(2)}, u32[]{:S(2)}) %collective-permute-start.26) | collective-permute-done | bytes 1048608 | tf_op jit(solution)/shard_map/ppermute | solution.py:123
  146.2 24.6 %collective-permute-done.4 = bf16[512,1152]{0,1:T(8,128)(2,1)S(1)} collective-permute-done((bf16[512,1152]{0,1:T(8,128)(2,1)}, bf16[512,1152]{0,1:T(8,128)(2,1)S(1)}, u32[]{:S(2)}, u32[]{:S(2)}) %collective-permute-start.4) | collective-permute-done | bytes 1179680 | tf_op jit(solution)/shard_map/ppermute | solution.py:123
  176.2 22.1 %collective-permute-done.7.refs_4_ = bf16[256,2048]{1,0:T(8,128)(2,1)S(1)} collective-permute-done((bf16[256,2048]{1,0:T(8,128)(2,1)S(1)}, bf16[256,2048]{1,0:T(8,128)(2,1)S(1)}, u32[]{:S(2)}, u32[]{:S(2)}) %collective-permute-start.7) | collective-permute-done | bytes 1048608 | tf_op jit(solution)/shard_map/ppermute | solution.py:123
  206.6 21.2 %collective-permute-done.8.refs_4_ = bf16[256,2048]{1,0:T(8,128)(2,1)S(1)} collective-permute-done((bf16[256,2048]{1,0:T(8,128)(2,1)S(1)}, bf16[256,2048]{1,0:T(8,128)(2,1)S(1)}, u32[]{:S(2)}, u32[]{:S(2)}) %collective-permute-start.8) | collective-permute-done | bytes 1048608 | tf_op jit(solution)/shard_map/ppermute | solution.py:123
  228.8 21.1 %collective-permute-done.28.refs_0_ = bf16[256,2048]{1,0:T(8,128)(2,1)S(1)} collective-permute-done((bf16[256,2048]{1,0:T(8,128)(2,1)S(1)}, bf16[256,2048]{1,0:T(8,128)(2,1)S(1)}, u32[]{:S(2)}, u32[]{:S(2)}) %collective-permute-start.28) | collective-permute-done | bytes 1048608 | tf_op jit(solution)/shard_map/ppermute | solution.py:123
  253.5 24.3 %collective-permute-done.9.refs_0_ = bf16[256,2048]{1,0:T(8,128)(2,1)S(1)} collective-permute-done((bf16[256,2048]{1,0:T(8,128)(2,1)S(1)}, bf16[256,2048]{1,0:T(8,128)(2,1)S(1)}, u32[]{:S(2)}, u32[]{:S(2)}) %collective-permute-start.9) | collective-permute-done | bytes 1048608 | tf_op jit(solution)/shard_map/ppermute | solution.py:123
  279.2 19.8 %collective-permute-done.29.refs_0_ = bf16[256,2048]{1,0:T(8,128)(2,1)} collective-permute-done((bf16[256,2048]{1,0:T(8,128)(2,1)S(1)}, bf16[256,2048]{1,0:T(8,128)(2,1)}, u32[]{:S(2)}, u32[]{:S(2)}) %collective-permute-start.29) | collective-permute-done | bytes 1048608 | tf_op jit(solution)/shard_map/ppermute | solution.py:123
  305.7 21.1 %collective-permute-done.10.refs_0_ = bf16[256,2048]{1,0:T(8,128)(2,1)S(1)} collective-permute-done((bf16[256,2048]{1,0:T(8,128)(2,1)S(1)}, bf16[256,2048]{1,0:T(8,128)(2,1)S(1)}, u32[]{:S(2)}, u32[]{:S(2)}) %collective-permute-start.10) | collective-permute-done | bytes 1048608 | tf_op jit(solution)/shard_map/ppermute | solution.py:123
  328.4 20.5 %collective-permute-done.30.refs_4_ = bf16[256,2048]{1,0:T(8,128)(2,1)S(1)} collective-permute-done((bf16[256,2048]{1,0:T(8,128)(2,1)S(1)}, bf16[256,2048]{1,0:T(8,128)(2,1)S(1)}, u32[]{:S(2)}, u32[]{:S(2)}) %collective-permute-start.30) | collective-permute-done | bytes 1048608 | tf_op jit(solution)/shard_map/ppermute | solution.py:123
  357.6 21.7 %collective-permute-done.40.refs_4_ = bf16[256,2048]{1,0:T(8,128)(2,1)} collective-permute-done((bf16[256,2048]{1,0:T(8,128)(2,1)S(1)}, bf16[256,2048]{1,0:T(8,128)(2,1)}, u32[]{:S(2)}, u32[]{:S(2)}) %collective-permute-start.40) | collective-permute-done | bytes 1048608 | tf_op jit(solution)/shard_map/ppermute | solution.py:123
  382.2 18.7 %collective-permute-done.31.refs_4_ = bf16[256,2048]{1,0:T(8,128)(2,1)} collective-permute-done((bf16[256,2048]{1,0:T(8,128)(2,1)}, bf16[256,2048]{1,0:T(8,128)(2,1)}, u32[]{:S(2)}, u32[]{:S(2)}) %collective-permute-start.31) | collective-permute-done | bytes 1048608 | tf_op jit(solution)/shard_map/ppermute | solution.py:123
  408.2 16.3 %product.10 = (f32[1152,8192]{1,0:T(8,128)}, f32[1,2048]{1,0:T(1,128)}) custom-call(s32[8]{0:T(128)S(1)} %stack.35.place_ref, bf16[1152,4096]{1,0:T(8,128)(2,1)} %bitcast.18, bf16[256,8192]{1,0:T(8,128)(2,1)S(1)} %copy-done, bf16[256,8192]{1,0:T(8,128)(2,1)} %collective-permute-done.11.refs_1_, bf16[256,8192]{1,0:T(8,128)(2,1)} %collective-permute-done.16.refs_2_, ...), custom_call_target="tpu_custom_call" | custom-call | flops 9663676416 | bytes 22544384 | tf_op jit(solution)/shard_map/product/pallas_call | solution.py:51
  426.6 16.3 %product.11 = (f32[1152,8192]{1,0:T(8,128)}, f32[1,2048]{1,0:T(1,128)}) custom-call(s32[8]{0:T(128)S(1)} %stack.35.place_ref, bf16[1152,4096]{1,0:T(8,128)(2,1)} %bitcast.19, bf16[256,8192]{1,0:T(8,128)(2,1)S(1)} %copy-done, bf16[256,8192]{1,0:T(8,128)(2,1)} %collective-permute-done.11.refs_1_, ...), custom_call_target="tpu_custom_call", output_to_operand_aliasing={{0}: (10, {})} | custom-call | flops 9663676416 | bytes 22544384 | tf_op jit(solution)/shard_map/product/pallas_call | solution.py:51
  443.9 16.1 %product.12 = (f32[1152,8192]{1,0:T(8,128)}, f32[1,2048]{1,0:T(1,128)}) custom-call(s32[8]{0:T(128)S(1)} %stack.35.place_ref, bf16[1152,4096]{1,0:T(8,128)(2,1)} %bitcast.20, bf16[256,8192]{1,0:T(8,128)(2,1)S(1)} %copy-done, bf16[256,8192]{1,0:T(8,128)(2,1)} %collective-permute-done.11.refs_1_, ...), custom_call_target="tpu_custom_call", output_to_operand_aliasing={{0}: (10, {})} | custom-call | flops 9663676416 | bytes 22544384 | tf_op jit(solution)/shard_map/product/pallas_call | solution.py:51
  460.1 16.4 %product.13 = (f32[1152,8192]{1,0:T(8,128)}, f32[1,2048]{1,0:T(1,128)}) custom-call(s32[8]{0:T(128)S(1)} %stack.35.place_ref, bf16[1152,4096]{1,0:T(8,128)(2,1)} %bitcast.21, bf16[256,8192]{1,0:T(8,128)(2,1)S(1)} %copy-done, bf16[256,8192]{1,0:T(8,128)(2,1)} %collective-permute-done.11.refs_1_, ...), custom_call_target="tpu_custom_call", output_to_operand_aliasing={{0}: (10, {})} | custom-call | flops 9663676416 | bytes 22544384 | tf_op jit(solution)/shard_map/product/pallas_call | solution.py:51
  478.9 17.9 %product.14 = (f32[1152,8192]{1,0:T(8,128)}, f32[1,2048]{1,0:T(1,128)S(1)}, f32[1152,128]{1,0:T(8,128)S(1)}) custom-call(s32[8]{0:T(128)S(1)} %stack.35.place_ref, bf16[1152,4096]{1,0:T(8,128)(2,1)} %bitcast.22, bf16[256,2048]{1,0:T(8,128)(2,1)S(1)} %copy-done.26, bf16[256,2048]{1,0:T(8,128)(2,1)S(1)} %copy-done.32, ...), custom_call_target="tpu_custom_call", output_to_operand_aliasing={{0}: (10, {})} | custom-call | flops 9663676416 | bytes 31981568 | tf_op jit(solution)/shard_map/product/pallas_call | solution.py:51
  498.4 17.5 %product.15 = (f32[1152,8192]{1,0:T(8,128)}, f32[1,2048]{1,0:T(1,128)S(1)}, f32[1152,128]{1,0:T(8,128)S(1)}) custom-call(s32[8]{0:T(128)S(1)} %stack.35.place_ref, bf16[1152,4096]{1,0:T(8,128)(2,1)} %bitcast.23, bf16[256,2048]{1,0:T(8,128)(2,1)S(1)} %copy-done.28, bf16[256,2048]{1,0:T(8,128)(2,1)S(1)} %copy-done.40, ...), custom_call_target="tpu_custom_call", output_to_operand_aliasing={{0}: (10, {})} | custom-call | flops 9663676416 | bytes 31981568 | tf_op jit(solution)/shard_map/product/pallas_call | solution.py:51
  531.7 8.4 %multiply_reduce_fusion = f32[1152]{0:T(1024)S(1)} fusion(f32[1152,8192]{1,0:T(8,128)} %get-tuple-element.155.refs_8_, f32[4096]{0:T(1024)S(1)} %get-tuple-element.186), kind=kLoop, calls=%fused_computation | loop fusion | flops 14154624 | bytes 18895360 | tf_op jit(solution)/shard_map/reduce_sum | solution.py:235
  541.9 17.9 %product.16 = (f32[1152,8192]{1,0:T(8,128)}, f32[1,2048]{1,0:T(1,128)S(1)}, f32[1152,128]{1,0:T(8,128)S(1)}) custom-call(s32[8]{0:T(128)S(1)} %stack.35.place_ref, bf16[1152,4096]{1,0:T(8,128)(2,1)} %bitcast.24, bf16[256,2048]{1,0:T(8,128)(2,1)} %collective-permute-done.29.refs_0_, ...), custom_call_target="tpu_custom_call", output_to_operand_aliasing={{0}: (10, {})} | custom-call | flops 9663676416 | bytes 31981568 | tf_op jit(solution)/shard_map/product/pallas_call | solution.py:51
  561.4 11.5 %product.17 = (f32[1152,8192]{1,0:T(8,128)}, f32[1,1024]{1,0:T(1,128)S(1)}, f32[1152,128]{1,0:T(8,128)S(1)}) custom-call(s32[8]{0:T(128)S(1)} %stack.35.place_ref, bf16[1152,4096]{1,0:T(8,128)(2,1)} %bitcast.25, bf16[256,2048]{1,0:T(8,128)(2,1)S(1)} %collective-permute-done.10.refs_0_, ...), custom_call_target="tpu_custom_call", output_to_operand_aliasing={{0}: (10, {})} | custom-call | flops 4831838208 | bytes 18350080 | tf_op jit(solution)/shard_map/product/pallas_call | solution.py:51
  601.0 8.1 %product.19 = (f32[1152,8192]{1,0:T(8,128)}, f32[1,512]{1,0:T(1,128)S(1)}, f32[1152,128]{1,0:T(8,128)S(1)}) custom-call(s32[8]{0:T(128)S(1)} %stack.35.place_ref, bf16[1152,4096]{1,0:T(8,128)(2,1)} %bitcast.27, bf16[256,2048]{1,0:T(8,128)(2,1)S(1)} %collective-permute-done.10.refs_0_, ...), custom_call_target="tpu_custom_call", output_to_operand_aliasing={{0}: (10, {})} | custom-call | flops 2415919104 | bytes 11534336 | tf_op jit(solution)/shard_map/product/pallas_call | solution.py:51
  637.5 47.2 %weight_step.1 = (f32[1152,8192]{1,0:T(8,128)}, bf16[1152,8192]{1,0:T(8,128)(2,1)}) custom-call(f32[1,1]{1,0:T(1,128)S(6)} %div.85.clip_ref, f32[1152,1]{1,0:T(8,128)S(1)} %broadcast_in_dim.16.row_ref, f32[1,8192]{1,0:T(1,128)S(1)} %maximum_rsqrt_fusion.col_ref, f32[1152,8192]{1,0:T(8,128)} %weight_ref.1, f32[1152,8192]{1,0:T(8,128)} %get-tuple-element.170.grad_ref), custom_call_target="tpu_custom_call" | custom-call | flops 47185920 | bytes 132120576 | tf_op jit(solution)/shard_map/weight_step/pallas_call | solution.py:92
  (320 shorter events, 155.8 us)
Async XLA Ops:
  11.8 79.2 %collective-permute-start.3 = (bf16[512,1152]{0,1:T(8,128)(2,1)}, bf16[512,1152]{0,1:T(8,128)(2,1)}, u32[]{:S(2)}, u32[]{:S(2)}) collective-permute-start(bf16[512,1152]{0,1:T(8,128)(2,1)} %copy.34), channel_id=1, source_target_pairs={{0,16},{8,24},{16,0},{24,8},{1,17},{9,25},{17,1},{25,9},{2,18},{10... | collective-permute-start | bytes 3538952 | tf_op jit(solution)/shard_map/ppermute | solution.py:123
  15.8 75.2 %collective-permute-start.1 = (bf16[512,1152]{0,1:T(8,128)(2,1)}, bf16[512,1152]{0,1:T(8,128)(2,1)S(1)}, u32[]{:S(2)}, u32[]{:S(2)}) collective-permute-start(bf16[512,1152]{0,1:T(8,128)(2,1)} %copy.33), channel_id=1, source_target_pairs={{0,8},{8,16},{16,24},{24,0},{1,9},{9,17},{17,25},{25,1},{2,10},{10... | collective-permute-start | bytes 3538952 | tf_op jit(solution)/shard_map/ppermute | solution.py:123
  17.3 182.6 %collective-permute-start.16 = (bf16[256,8192]{1,0:T(8,128)(2,1)}, bf16[256,8192]{1,0:T(8,128)(2,1)}, u32[]{:S(2)}, u32[]{:S(2)}) collective-permute-start(bf16[256,8192]{1,0:T(8,128)(2,1)} %refs_0_.7), channel_id=1, source_target_pairs={{0,4},{2,6},{4,0},{6,2},{1,5},{3,7},{5,1},{7,3},{8,12},{10,14},{12... | collective-permute-start | bytes 12582920 | tf_op jit(solution)/shard_map/ppermute | solution.py:123
  18.8 181.2 %collective-permute-start.11 = (bf16[256,8192]{1,0:T(8,128)(2,1)}, bf16[256,8192]{1,0:T(8,128)(2,1)}, u32[]{:S(2)}, u32[]{:S(2)}) collective-permute-start(bf16[256,8192]{1,0:T(8,128)(2,1)} %refs_0_.7), channel_id=1, source_target_pairs={{0,2},{2,0},{4,6},{6,4},{1,3},{3,1},{5,7},{7,5},{8,10},{10,8},{12,... | collective-permute-start | bytes 12582920 | tf_op jit(solution)/shard_map/ppermute | solution.py:123
  91.0 52.9 %collective-permute-start.5 = (bf16[512,1152]{0,1:T(8,128)(2,1)S(1)}, bf16[512,1152]{0,1:T(8,128)(2,1)S(1)}, u32[]{:S(2)}, u32[]{:S(2)}) collective-permute-start(bf16[512,1152]{0,1:T(8,128)(2,1)S(1)} %copy-done.57), channel_id=1, source_target_pairs={{0,24},{8,0},{16,8},{24,16},{1,25},{9,1},{17,9},{25,17},{2,26},{10... | collective-permute-start | bytes 3538952 | tf_op jit(solution)/shard_map/ppermute | solution.py:123
  91.0 52.4 %collective-permute-start.26 = (bf16[256,2048]{1,0:T(8,128)(2,1)S(1)}, bf16[256,2048]{1,0:T(8,128)(2,1)S(1)}, u32[]{:S(2)}, u32[]{:S(2)}) collective-permute-start(bf16[256,2048]{1,0:T(8,128)(2,1)S(1)} %get-tuple-element.111), channel_id=1, source_target_pairs={{0,8},{8,16},{16,24},{24,0},{1,9},{9,17},{17,25},{25,1},{2,10},{10... | collective-permute-start | bytes 3145736 | tf_op jit(solution)/shard_map/ppermute | solution.py:123
  93.0 50.9 %collective-permute-start.2 = (bf16[512,1152]{0,1:T(8,128)(2,1)S(1)}, bf16[512,1152]{0,1:T(8,128)(2,1)S(1)}, u32[]{:S(2)}, u32[]{:S(2)}) collective-permute-start(bf16[512,1152]{0,1:T(8,128)(2,1)S(1)} %collective-permute-done.1), channel_id=1, source_target_pairs={{0,1},{1,0},{2,3},{3,2},{4,5},{5,4},{6,7},{7,6},{8,9},{9,8},{10,11... | collective-permute-start | bytes 3538952 | tf_op jit(solution)/shard_map/ppermute | solution.py:123
  200.1 126.8 %collective-permute-start.21 = (bf16[256,8192]{1,0:T(8,128)(2,1)}, bf16[256,8192]{1,0:T(8,128)(2,1)S(1)}, u32[]{:S(2)}, u32[]{:S(2)}) collective-permute-start(bf16[256,8192]{1,0:T(8,128)(2,1)} %collective-permute-done.16.refs_2_), channel_id=1, source_target_pairs={{0,2},{2,0},{4,6},{6,4},{1,3},{3,1},{5,7},{7,5},{8,10},{10,8},{12,... | collective-permute-start | bytes 12582920 | tf_op jit(solution)/shard_map/ppermute | solution.py:123
  204.1 45.8 %collective-permute-start.28 = (bf16[256,2048]{1,0:T(8,128)(2,1)S(1)}, bf16[256,2048]{1,0:T(8,128)(2,1)S(1)}, u32[]{:S(2)}, u32[]{:S(2)}) collective-permute-start(bf16[256,2048]{1,0:T(8,128)(2,1)S(1)} %collective-permute-done.26.refs_4_), channel_id=1, source_target_pairs={{0,8},{8,16},{16,24},{24,0},{1,9},{9,17},{17,25},{25,1},{2,10},{10... | collective-permute-start | bytes 3145736 | tf_op jit(solution)/shard_map/ppermute | solution.py:123
  204.1 45.8 %collective-permute-start.17 = (bf16[256,2048]{1,0:T(8,128)(2,1)S(1)}, bf16[256,2048]{1,0:T(8,128)(2,1)S(1)}, u32[]{:S(2)}, u32[]{:S(2)}) collective-permute-start(bf16[256,2048]{1,0:T(8,128)(2,1)S(1)} %collective-permute-done.7.refs_4_), channel_id=1, source_target_pairs={{0,4},{2,6},{4,0},{6,2},{1,5},{3,7},{5,1},{7,3},{8,12},{10,14},{12... | collective-permute-start | bytes 3145736 | tf_op jit(solution)/shard_map/ppermute | solution.py:123
  249.9 49.2 %collective-permute-start.29 = (bf16[256,2048]{1,0:T(8,128)(2,1)S(1)}, bf16[256,2048]{1,0:T(8,128)(2,1)}, u32[]{:S(2)}, u32[]{:S(2)}) collective-permute-start(bf16[256,2048]{1,0:T(8,128)(2,1)S(1)} %collective-permute-done.27.refs_4_), channel_id=1, source_target_pairs={{0,8},{8,16},{16,24},{24,0},{1,9},{9,17},{17,25},{25,1},{2,10},{10... | collective-permute-start | bytes 3145736 | tf_op jit(solution)/shard_map/ppermute | solution.py:123
  251.0 48.1 %collective-permute-start.46 = (bf16[256,2048]{1,0:T(8,128)(2,1)S(1)}, bf16[256,2048]{1,0:T(8,128)(2,1)S(1)}, u32[]{:S(2)}, u32[]{:S(2)}) collective-permute-start(bf16[256,2048]{1,0:T(8,128)(2,1)S(1)} %collective-permute-done.28.refs_0_), channel_id=1, source_target_pairs={{0,4},{2,6},{4,0},{6,2},{1,5},{3,7},{5,1},{7,3},{8,12},{10,14},{12... | collective-permute-start | bytes 3145736 | tf_op jit(solution)/shard_map/ppermute | solution.py:123
  253.5 46.6 %collective-permute-start.35 = (bf16[256,2048]{1,0:T(8,128)(2,1)S(1)}, bf16[256,2048]{1,0:T(8,128)(2,1)S(1)}, u32[]{:S(2)}, u32[]{:S(2)}) collective-permute-start(bf16[256,2048]{1,0:T(8,128)(2,1)S(1)} %collective-permute-done.28.refs_0_), channel_id=1, source_target_pairs={{0,2},{2,0},{4,6},{6,4},{1,3},{3,1},{5,7},{7,5},{8,10},{10,8},{12,... | collective-permute-start | bytes 3145736 | tf_op jit(solution)/shard_map/ppermute | solution.py:123
  301.0 47.9 %collective-permute-start.30 = (bf16[256,2048]{1,0:T(8,128)(2,1)S(1)}, bf16[256,2048]{1,0:T(8,128)(2,1)S(1)}, u32[]{:S(2)}, u32[]{:S(2)}) collective-permute-start(bf16[256,2048]{1,0:T(8,128)(2,1)S(1)} %collective-permute-done.28.refs_0_), channel_id=1, source_target_pairs={{0,8},{8,16},{16,24},{24,0},{1,9},{9,17},{17,25},{25,1},{2,10},{10... | collective-permute-start | bytes 3145736 | tf_op jit(solution)/shard_map/ppermute | solution.py:123
  302.0 47.9 %collective-permute-start.50 = (bf16[256,2048]{1,0:T(8,128)(2,1)}, bf16[256,2048]{1,0:T(8,128)(2,1)}, u32[]{:S(2)}, u32[]{:S(2)}) collective-permute-start(bf16[256,2048]{1,0:T(8,128)(2,1)} %collective-permute-done.29.refs_0_), channel_id=1, source_target_pairs={{0,4},{2,6},{4,0},{6,2},{1,5},{3,7},{5,1},{7,3},{8,12},{10,14},{12... | collective-permute-start | bytes 3145736 | tf_op jit(solution)/shard_map/ppermute | solution.py:123
  304.5 45.9 %collective-permute-start.49 = (bf16[256,2048]{1,0:T(8,128)(2,1)S(1)}, bf16[256,2048]{1,0:T(8,128)(2,1)S(1)}, u32[]{:S(2)}, u32[]{:S(2)}) collective-permute-start(bf16[256,2048]{1,0:T(8,128)(2,1)S(1)} %collective-permute-done.46.refs_2_), channel_id=1, source_target_pairs={{0,2},{2,0},{4,6},{6,4},{1,3},{3,1},{5,7},{7,5},{8,10},{10,8},{12,... | collective-permute-start | bytes 3145736 | tf_op jit(solution)/shard_map/ppermute | solution.py:123
  379.3 45.2 %collective-permute-start.20 = (bf16[256,2048]{1,0:T(8,128)(2,1)S(1)}, bf16[256,2048]{1,0:T(8,128)(2,1)S(1)}, u32[]{:S(2)}, u32[]{:S(2)}) collective-permute-start(bf16[256,2048]{1,0:T(8,128)(2,1)S(1)} %collective-permute-done.10.refs_0_), channel_id=1, source_target_pairs={{0,4},{2,6},{4,0},{6,2},{1,5},{3,7},{5,1},{7,3},{8,12},{10,14},{12... | collective-permute-start | bytes 3145736 | tf_op jit(solution)/shard_map/ppermute | solution.py:123
  381.7 96.6 %collective-permute-start.37 = (bf16[256,2048]{1,0:T(8,128)(2,1)}, bf16[256,2048]{1,0:T(8,128)(2,1)}, u32[]{:S(2)}, u32[]{:S(2)}) collective-permute-start(bf16[256,2048]{1,0:T(8,128)(2,1)} %copy-done.33), channel_id=1, source_target_pairs={{0,2},{2,0},{4,6},{6,4},{1,3},{3,1},{5,7},{7,5},{8,10},{10,8},{12,... | collective-permute-start | bytes 3145736 | tf_op jit(solution)/shard_map/ppermute | solution.py:123
  400.9 95.9 %collective-permute-start.58 = (bf16[256,1024]{1,0:T(8,128)(2,1)S(1)}, bf16[256,1024]{1,0:T(8,128)(2,1)}, u32[]{:S(2)}, u32[]{:S(2)}) collective-permute-start(bf16[256,1024]{1,0:T(8,128)(2,1)S(1)} %slice.71), channel_id=1, source_target_pairs={{0,8},{8,16},{16,24},{24,0},{1,9},{9,17},{17,25},{25,1},{2,10},{10... | collective-permute-start | bytes 1572872 | tf_op jit(solution)/shard_map/ppermute | solution.py:123
  424.5 54.0 %collective-permute-start.53 = (bf16[256,2048]{1,0:T(8,128)(2,1)}, bf16[256,2048]{1,0:T(8,128)(2,1)}, u32[]{:S(2)}, u32[]{:S(2)}) collective-permute-start(bf16[256,2048]{1,0:T(8,128)(2,1)} %collective-permute-done.51.refs_6_), channel_id=1, source_target_pairs={{0,2},{2,0},{4,6},{6,4},{1,3},{3,1},{5,7},{7,5},{8,10},{10,8},{12,... | collective-permute-start | bytes 3145736 | tf_op jit(solution)/shard_map/ppermute | solution.py:123
  425.1 51.4 %collective-permute-start.42 = (bf16[256,2048]{1,0:T(8,128)(2,1)}, bf16[256,2048]{1,0:T(8,128)(2,1)}, u32[]{:S(2)}, u32[]{:S(2)}) collective-permute-start(bf16[256,2048]{1,0:T(8,128)(2,1)} %collective-permute-done.40.refs_4_), channel_id=1, source_target_pairs={{0,4},{2,6},{4,0},{6,2},{1,5},{3,7},{5,1},{7,3},{8,12},{10,14},{12... | collective-permute-start | bytes 3145736 | tf_op jit(solution)/shard_map/ppermute | solution.py:123
  476.5 53.4 %collective-permute-start.54 = (bf16[256,2048]{1,0:T(8,128)(2,1)}, bf16[256,2048]{1,0:T(8,128)(2,1)}, u32[]{:S(2)}, u32[]{:S(2)}) collective-permute-start(bf16[256,2048]{1,0:T(8,128)(2,1)} %collective-permute-done.31.refs_4_), channel_id=1, source_target_pairs={{0,4},{2,6},{4,0},{6,2},{1,5},{3,7},{5,1},{7,3},{8,12},{10,14},{12... | collective-permute-start | bytes 3145736 | tf_op jit(solution)/shard_map/ppermute | solution.py:123
  478.1 52.5 %collective-permute-start.32 = (bf16[256,512]{1,0:T(8,128)(2,1)}, bf16[256,512]{1,0:T(8,128)(2,1)S(1)}, u32[]{:S(2)}, u32[]{:S(2)}) collective-permute-start(bf16[256,512]{1,0:T(8,128)(2,1)} %get-tuple-element.118), channel_id=1, source_target_pairs={{0,8},{8,16},{16,24},{24,0},{1,9},{9,17},{17,25},{25,1},{2,10},{10... | collective-permute-start | bytes 786440 | tf_op jit(solution)/shard_map/ppermute | solution.py:123
  540.1 45.2 %collective-permute-start.55 = (bf16[256,512]{1,0:T(8,128)(2,1)S(1)}, bf16[256,512]{1,0:T(8,128)(2,1)S(1)}, u32[]{:S(2)}, u32[]{:S(2)}) collective-permute-start(bf16[256,512]{1,0:T(8,128)(2,1)S(1)} %collective-permute-done.32.refs_4_), channel_id=1, source_target_pairs={{0,4},{2,6},{4,0},{6,2},{1,5},{3,7},{5,1},{7,3},{8,12},{10,14},{12... | collective-permute-start | bytes 786440 | tf_op jit(solution)/shard_map/ppermute | solution.py:123
  (117 other events, 2178.1 us)

commit v3 on v2

--- a/solution.py
+++ b/solution.py
@@ -112,23 +112,12 @@
     )(inverse_clip.reshape(1, 1), row_scale[:, None], col_scale[None, :], weight, grad)
 
 
-class Lane:
-    def __init__(self, axis, size, ahead):
-        self.axis, self.size, self.ahead, self.sent = axis, size, ahead, []
-
-    def send(self, value, target, after=()):
-        value = lax.optimization_barrier((value, *after))[0] if after else value
-        if len(self.sent) >= self.ahead:
-            value, _ = lax.optimization_barrier((value, self.sent[-self.ahead]))
-        value = lax.ppermute(value, self.axis, [(i, target(i)) for i in range(self.size)])
-        self.sent.append(value)
-        return value
-
-    def shift(self, value, by, after=()):
-        return self.send(value, lambda i: (i + by) % self.size, after)
-
-    def flip(self, value, bit):
-        return self.send(value, lambda i: i ^ bit)
+def shifted(value, axis, size, by):
+    return lax.ppermute(value, axis, [(i, (i + by) % size) for i in range(size)])
+
+
+def flipped(value, axis, size):
+    return lax.ppermute(value, axis, [(i, i ^ 1) for i in range(size)])
 
 
 def total(value, axis, size):
@@ -149,24 +138,23 @@
     relative = min(0.01, float(STEP) ** (-0.5))
     rows = weight.shape[0]
     columns = cotangent.shape[1]
-    along_z, along_x, along_y, cores = Lane("dp", n_dp, 2), Lane("row", n_row, 2), Lane("col", n_col, 2), Lane("row", n_row, 4)
 
     def over_rows(value):
         return total(total(value, "row", n_row), "dp", n_dp)
 
     own = []
     for u in range(n_x):
-        across = along_x.shift(cotangent, 2 * u) if u else cotangent
-        own += [across, cores.flip(across, 1)]
+        across = shifted(cotangent, "row", n_row, 2 * u) if u else cotangent
+        own += [across, flipped(across, "row", n_row)]
 
     pieces = []
     for s in range(n_dp):
         to = lax.rem(z + s, n_dp)
         piece = lax.dynamic_slice_in_dim(activations, to * rows, rows, axis=1)
-        pieces.append(along_z.shift(piece, s) if s else piece)
+        pieces.append(shifted(piece, "dp", n_dp, s) if s else piece)
     act = []
     for piece in pieces:
-        parts = [along_y.shift(piece, t) if t else piece for t in range(n_col)]
+        parts = [shifted(piece, "col", n_col, t) if t else piece for t in range(n_col)]
         ordered = [parts[0]] * n_col
         for at in range(n_col):
             for t in range(1, n_col):
@@ -188,11 +176,45 @@
         return [(sum(widths[:k]), width) for k, width in enumerate(widths)]
 
     moving = [(start, cotangent[:, start : start + width]) for start, width in cut(SHARES)]
-    first_half, second_half = [(block, 0) for block in own], []
-    grad, row_lanes, weighted, col_new = None, 0.0, 0.0, []
-    first_done, col_sums, lasts = [], [], cut(LAST_SHARES)
+    first_half = [(block, 0) for block in own]
+    grad, row_lanes, weighted, col_new, col_sums = None, 0.0, 0.0, [], []
+    lasts = cut(LAST_SHARES)
     starts = [start for start, _ in lasts]
-    count = 0
+
+    def finish(k, act, grad):
+        nonlocal row_lanes, weighted
+        start, width = lasts[k]
+        blocks = [
+            block
+            for s, at, size, held, _ in arrivals
+            if s >= half and at <= start < at + size
+            for block in held
+        ]
+        grad, col_part, row_part = product(act, 1, places, blocks, start, width, grad, columns)
+        row_lanes = row_lanes + row_part
+        col_sums.append(col_part)
+        if k in (1, 3):
+            low, high = starts[k - 1], start + width
+            col_sum = jnp.concatenate(col_sums[k - 1 : k + 1], axis=1)
+            col_new.append(decay_rate * col_moment[low:high] + (1.0 - decay_rate) * over_rows(col_sum)[0] / D)
+            squared = jnp.square(grad[:, low:high])
+            weighted = weighted + jnp.sum(squared * (1.0 / col_new[-1])[None, :], axis=1)
+            grad, weighted = lax.optimization_barrier((grad, weighted))
+        return grad
+
+    arrivals = []
+    settled = 0
+
+    def settle(tied):
+        nonlocal settled
+        _, start, _, blocks, crossed = arrivals[settled]
+        settled += 1
+        if crossed and tied is not None:
+            tied, *crossed = lax.optimization_barrier((tied, *crossed))
+        for across in crossed:
+            blocks += [(across, start), (flipped(across, "row", n_row), start)]
+        return tied
+
     for s in range(1, n_dp):
         last = s == n_dp - 1
         if last:
@@ -202,38 +224,26 @@
                 for k, (at, width) in zip(holders, lasts)
             ]
         for k, (start, block) in enumerate(moving):
-            width = block.shape[1]
-            after = ()
-            if s >= half:
-                after = (first_done[count - 2],) if 0 <= count - 2 < len(first_done) else (act,) if count == 0 else ()
-                count += 1
-            block = along_z.shift(block, 1, after)
+            at = len(arrivals)
+            if at >= 3:
+                block = settle(block)
+            count = at - len(SHARES) * (half - 1)
+            if 2 <= count < 2 + len(SHARES):
+                _, first, width, blocks, _ = arrivals[len(SHARES) * (half - 2) + count - 2]
+                grad = product(act, 0, places, first_half + blocks, first, width, grad, columns)[0]
+                block, grad = lax.optimization_barrier((block, grad))
+            block = shifted(block, "dp", n_dp, 1)
             moving[k] = (start, block)
-            arrived = []
-            for u in range(n_x):
-                after = (col_sums[k - 3],) if last and u and k >= 3 else ()
-                across = along_x.shift(block, 2 * u, after) if u else block
-                arrived += [(across, start), (cores.flip(across, 1), start)]
-            if s < half:
-                first_half_here = first_half + arrived
-                grad, token = product(act, 0, places, first_half_here, start, width, grad, columns)
-                first_done.append(token)
-            elif not last:
-                second_half.append((start, width, arrived))
-            else:
-                earlier = [b for at, size, blocks in second_half if at <= start < at + size for b in blocks]
-                grad, col_part, row_part = product(act, 1, places, earlier + arrived, start, width, grad, columns)
-                row_lanes = row_lanes + row_part
-                col_sums.append(col_part)
-            if last and (k == 1 or k == 3):
-                low, high = starts[k - 1], start + width
-                col_sum = jnp.concatenate(col_sums[k - 1 : k + 1], axis=1)
-                col_new.append(
-                    decay_rate * col_moment[low:high] + (1.0 - decay_rate) * over_rows(col_sum)[0] / D
-                )
-                squared = jnp.square(grad[:, low:high])
-                weighted = weighted + jnp.sum(squared * (1.0 / col_new[-1])[None, :], axis=1)
-                grad, weighted = lax.optimization_barrier((grad, weighted))
+            if last and k >= 3:
+                grad = finish(k - 3, act, grad)
+                block, grad = lax.optimization_barrier((block, grad))
+            blocks = [(block, start), (flipped(block, "row", n_row), start)]
+            crossed = [shifted(block, "row", n_row, 2 * u) for u in range(1, n_x)]
+            arrivals.append((s, start, block.shape[1], blocks, crossed))
+    while settled < len(arrivals):
+        settle(None)
+    for k in range(len(lasts) - 3, len(lasts)):
+        grad = finish(k, act, grad)
     low, high = starts[4], columns
     col_sum = jnp.concatenate(col_sums[4:], axis=1)
     squared = jnp.square(grad[:, low:high])

time: 692 us -> 676 us (0.977)
  local copies, waits for them, and re-layouts: 43.5 us -> 32.3 us
    unnamed x127 -> x52, local copies, waits for them, and re-layouts: 34.1 us -> 22.2 us
  transfers between devices with their start and end apart: 80 -> 80, of which waited for: 29 -> 33; matrix products, arithmetic and copies ran while one was open for 4% -> 6% of each run, Pallas kernels for 20% -> 19%
where the time goes in v3:
time: 676 us; the launch traced here: 669 us
  waiting for transfers between devices  359 us (53%)
  Pallas kernels  191 us (28%)
  starting transfers between devices  53.1 us (8%)
  local copies, waits for them, and re-layouts  32.3 us (5%)
  other arithmetic  28.6 us (4%)
    ppermute x36, waiting for transfers between devices, shifted(): lax.ppermute(value, axis, [(i, (i + by) % size) for i in range(size)])  329 us
    pallas_call x10, Pallas kernels, product(): pl.pallas_call(functools.partial(product_kernel, len(blocks), adds), grid...  144 us
    pallas_call x1, Pallas kernels, weight_step(): pl.pallas_call(functools.partial(step_kernel, relative), grid=(rows // ti...  47.2 us
    ppermute x36, starting transfers between devices, shifted(): lax.ppermute(value, axis, [(i, (i + by) % size) for i in range(size)])  34.4 us
    ppermute x14, waiting for transfers between devices, total(): lax.ppermute(value, axis, [(i, i ^ bit) for i in range(size)])  30.2 us
    unnamed x52, local copies, waits for them, and re-layouts  22.2 us
    reduce_sum x2, other arithmetic, finish(): jnp.sum(squared * (1.0 / col_new[-1])[None, :], axis=1)  14.9 us
  transfers between devices with their start and end apart: 80, of which 33 were waited for; matrix products, arithmetic and copies ran while one was open for 6% of the time, Pallas kernels for 19%

profile of v3, /device:TPU:0, one launch (start us, length us, event | category | flops | bytes accessed | tf_op | source)
XLA Modules:
  0.0 668.7 jit_solution(16155271246490519398)
XLA Ops:
  22.9 13.3 %collective-permute-done.7.refs_4_ = bf16[256,2048]{1,0:T(8,128)(2,1)} collective-permute-done((bf16[256,2048]{1,0:T(8,128)(2,1)}, bf16[256,2048]{1,0:T(8,128)(2,1)}, u32[]{:S(2)}, u32[]{:S(2)}) %collective-permute-start.7) | collective-permute-done | bytes 1048608 | tf_op jit(solution)/shard_map/ppermute | solution.py:116
  38.6 20.0 %collective-permute-done.19.refs_4_ = bf16[256,2048]{1,0:T(8,128)(2,1)S(1)} collective-permute-done((bf16[256,2048]{1,0:T(8,128)(2,1)}, bf16[256,2048]{1,0:T(8,128)(2,1)S(1)}, u32[]{:S(2)}, u32[]{:S(2)}) %collective-permute-start.19) | collective-permute-done | bytes 1048608 | tf_op jit(solution)/shard_map/ppermute | solution.py:116
  59.4 21.8 %collective-permute-done.10.refs_4_ = bf16[256,2048]{1,0:T(8,128)(2,1)S(1)} collective-permute-done((bf16[256,2048]{1,0:T(8,128)(2,1)}, bf16[256,2048]{1,0:T(8,128)(2,1)S(1)}, u32[]{:S(2)}, u32[]{:S(2)}) %collective-permute-start.10) | collective-permute-done | bytes 1048608 | tf_op jit(solution)/shard_map/ppermute | solution.py:116
  83.2 23.4 %collective-permute-done.1 = bf16[512,1152]{0,1:T(8,128)(2,1)} collective-permute-done((bf16[512,1152]{0,1:T(8,128)(2,1)}, bf16[512,1152]{0,1:T(8,128)(2,1)}, u32[]{:S(2)}, u32[]{:S(2)}) %collective-permute-start.1) | collective-permute-done | bytes 1179680 | tf_op jit(solution)/shard_map/ppermute | solution.py:116
  109.3 46.3 %collective-permute-done.3 = bf16[512,1152]{0,1:T(8,128)(2,1)} collective-permute-done((bf16[512,1152]{0,1:T(8,128)(2,1)}, bf16[512,1152]{0,1:T(8,128)(2,1)}, u32[]{:S(2)}, u32[]{:S(2)}) %collective-permute-start.3) | collective-permute-done | bytes 1179680 | tf_op jit(solution)/shard_map/ppermute | solution.py:116
  164.0 19.7 %collective-permute-done.5 = bf16[512,1152]{0,1:T(8,128)(2,1)S(1)} collective-permute-done((bf16[512,1152]{0,1:T(8,128)(2,1)}, bf16[512,1152]{0,1:T(8,128)(2,1)S(1)}, u32[]{:S(2)}, u32[]{:S(2)}) %collective-permute-start.5) | collective-permute-done | bytes 1179680 | tf_op jit(solution)/shard_map/ppermute | solution.py:116
  189.0 23.7 %collective-permute-done.4 = bf16[512,1152]{0,1:T(8,128)(2,1)S(1)} collective-permute-done((bf16[512,1152]{0,1:T(8,128)(2,1)}, bf16[512,1152]{0,1:T(8,128)(2,1)S(1)}, u32[]{:S(2)}, u32[]{:S(2)}) %collective-permute-start.4) | collective-permute-done | bytes 1179680 | tf_op jit(solution)/shard_map/ppermute | solution.py:116
  214.4 21.8 %collective-permute-done.6 = bf16[512,1152]{0,1:T(8,128)(2,1)S(1)} collective-permute-done((bf16[512,1152]{0,1:T(8,128)(2,1)S(1)}, bf16[512,1152]{0,1:T(8,128)(2,1)S(1)}, u32[]{:S(2)}, u32[]{:S(2)}) %collective-permute-start.6) | collective-permute-done | bytes 1179680 | tf_op jit(solution)/shard_map/ppermute | solution.py:116
  237.6 23.7 %collective-permute-done.29.refs_0_ = bf16[256,2048]{1,0:T(8,128)(2,1)S(1)} collective-permute-done((bf16[256,2048]{1,0:T(8,128)(2,1)S(1)}, bf16[256,2048]{1,0:T(8,128)(2,1)S(1)}, u32[]{:S(2)}, u32[]{:S(2)}) %collective-permute-start.29) | collective-permute-done | bytes 1048608 | tf_op jit(solution)/shard_map/ppermute | solution.py:116
  271.7 16.1 %product.10 = (f32[1152,8192]{1,0:T(8,128)}, f32[1,2048]{1,0:T(1,128)}) custom-call(s32[8]{0:T(128)S(1)} %stack.35.place_ref, bf16[1152,4096]{1,0:T(8,128)(2,1)} %bitcast.18, bf16[256,8192]{1,0:T(8,128)(2,1)S(1)} %copy-done, bf16[256,8192]{1,0:T(8,128)(2,1)} %copy-done.16, bf16[256,8192]{1,0:T(8,128)(2,1)} %collective-permute-done.15.refs_2_, ...), custom_call_target="tpu_custom_call" | custom-call | flops 9663676416 | bytes 22544384 | tf_op jit(solution)/shard_map/product/pallas_call | solution.py:51
  288.0 18.1 %collective-permute-done.33.refs_2_ = bf16[256,2048]{1,0:T(8,128)(2,1)S(1)} collective-permute-done((bf16[256,2048]{1,0:T(8,128)(2,1)S(1)}, bf16[256,2048]{1,0:T(8,128)(2,1)S(1)}, u32[]{:S(2)}, u32[]{:S(2)}) %collective-permute-start.33) | collective-permute-done | bytes 1048608 | tf_op jit(solution)/shard_map/ppermute | solution.py:116
  307.7 16.1 %product.11 = (f32[1152,8192]{1,0:T(8,128)}, f32[1,2048]{1,0:T(1,128)}) custom-call(s32[8]{0:T(128)S(1)} %stack.35.place_ref, bf16[1152,4096]{1,0:T(8,128)(2,1)} %bitcast.19, bf16[256,8192]{1,0:T(8,128)(2,1)S(1)} %copy-done, bf16[256,8192]{1,0:T(8,128)(2,1)} %copy-done.16, ...), custom_call_target="tpu_custom_call", output_to_operand_aliasing={{0}: (10, {})} | custom-call | flops 9663676416 | bytes 22544384 | tf_op jit(solution)/shard_map/product/pallas_call | solution.py:51
  324.4 16.0 %product.12 = (f32[1152,8192]{1,0:T(8,128)}, f32[1,2048]{1,0:T(1,128)}) custom-call(s32[8]{0:T(128)S(1)} %stack.35.place_ref, bf16[1152,4096]{1,0:T(8,128)(2,1)} %bitcast.20, bf16[256,8192]{1,0:T(8,128)(2,1)S(1)} %copy-done, bf16[256,8192]{1,0:T(8,128)(2,1)} %copy-done.16, ...), custom_call_target="tpu_custom_call", output_to_operand_aliasing={{0}: (10, {})} | custom-call | flops 9663676416 | bytes 22544384 | tf_op jit(solution)/shard_map/product/pallas_call | solution.py:51
  340.5 16.1 %product.13 = (f32[1152,8192]{1,0:T(8,128)}, f32[1,2048]{1,0:T(1,128)}) custom-call(s32[8]{0:T(128)S(1)} %stack.35.place_ref, bf16[1152,4096]{1,0:T(8,128)(2,1)} %bitcast.21, bf16[256,8192]{1,0:T(8,128)(2,1)S(1)} %copy-done, bf16[256,8192]{1,0:T(8,128)(2,1)} %copy-done.16, ...), custom_call_target="tpu_custom_call", output_to_operand_aliasing={{0}: (10, {})} | custom-call | flops 9663676416 | bytes 22544384 | tf_op jit(solution)/shard_map/product/pallas_call | solution.py:51
  359.5 8.8 %collective-permute-done.43.refs_4_ = bf16[256,2048]{1,0:T(8,128)(2,1)S(1)} collective-permute-done((bf16[256,2048]{1,0:T(8,128)(2,1)S(1)}, bf16[256,2048]{1,0:T(8,128)(2,1)S(1)}, u32[]{:S(2)}, u32[]{:S(2)}) %collective-permute-start.43) | collective-permute-done | bytes 1048608 | tf_op jit(solution)/shard_map/ppermute | solution.py:116
  369.8 21.0 %collective-permute-done.23.refs_0_ = bf16[256,2048]{1,0:T(8,128)(2,1)S(1)} collective-permute-done((bf16[256,2048]{1,0:T(8,128)(2,1)S(1)}, bf16[256,2048]{1,0:T(8,128)(2,1)S(1)}, u32[]{:S(2)}, u32[]{:S(2)}) %collective-permute-start.23) | collective-permute-done | bytes 1048608 | tf_op jit(solution)/shard_map/ppermute | solution.py:116
  392.2 19.8 %collective-permute-done.36.refs_4_ = bf16[256,2048]{1,0:T(8,128)(2,1)S(1)} collective-permute-done((bf16[256,2048]{1,0:T(8,128)(2,1)S(1)}, bf16[256,2048]{1,0:T(8,128)(2,1)S(1)}, u32[]{:S(2)}, u32[]{:S(2)}) %collective-permute-start.36) | collective-permute-done | bytes 1048608 | tf_op jit(solution)/shard_map/ppermute | solution.py:116
  414.2 21.7 %collective-permute-done.37.refs_6_ = bf16[256,2048]{1,0:T(8,128)(2,1)S(1)} collective-permute-done((bf16[256,2048]{1,0:T(8,128)(2,1)S(1)}, bf16[256,2048]{1,0:T(8,128)(2,1)S(1)}, u32[]{:S(2)}, u32[]{:S(2)}) %collective-permute-start.37) | collective-permute-done | bytes 1048608 | tf_op jit(solution)/shard_map/ppermute | solution.py:116
  439.2 17.4 %product.14 = (f32[1152,8192]{1,0:T(8,128)}, f32[1,2048]{1,0:T(1,128)S(1)}, f32[1152,128]{1,0:T(8,128)S(1)}) custom-call(s32[8]{0:T(128)S(1)} %stack.35.place_ref, bf16[1152,4096]{1,0:T(8,128)(2,1)} %bitcast.22, bf16[256,2048]{1,0:T(8,128)(2,1)S(1)} %collective-permute-done.12.refs_0_, ...), custom_call_target="tpu_custom_call", output_to_operand_aliasing={{0}: (10, {})} | custom-call | flops 9663676416 | bytes 31981568 | tf_op jit(solution)/shard_map/product/pallas_call | solution.py:51
  465.0 17.5 %product.15 = (f32[1152,8192]{1,0:T(8,128)}, f32[1,2048]{1,0:T(1,128)S(1)}, f32[1152,128]{1,0:T(8,128)S(1)}) custom-call(s32[8]{0:T(128)S(1)} %stack.35.place_ref, bf16[1152,4096]{1,0:T(8,128)(2,1)} %bitcast.23, bf16[256,2048]{1,0:T(8,128)(2,1)S(1)} %collective-permute-done.29.refs_0_, ...), custom_call_target="tpu_custom_call", output_to_operand_aliasing={{0}: (10, {})} | custom-call | flops 9663676416 | bytes 31981568 | tf_op jit(solution)/shard_map/product/pallas_call | solution.py:51
  503.8 8.4 %multiply_reduce_fusion = f32[1152]{0:T(1024)S(1)} fusion(f32[1152,8192]{1,0:T(8,128)} %get-tuple-element.110.refs_8_, f32[4096]{0:T(1024)S(1)} %get-tuple-element.138), kind=kLoop, calls=%fused_computation | loop fusion | flops 14154624 | bytes 18895360 | tf_op jit(solution)/shard_map/reduce_sum | solution.py:201
  517.7 17.7 %product.16 = (f32[1152,8192]{1,0:T(8,128)}, f32[1,2048]{1,0:T(1,128)S(1)}, f32[1152,128]{1,0:T(8,128)S(1)}) custom-call(s32[8]{0:T(128)S(1)} %stack.35.place_ref, bf16[1152,4096]{1,0:T(8,128)(2,1)} %bitcast.24, bf16[256,2048]{1,0:T(8,128)(2,1)} %collective-permute-done.25.refs_0_, ...), custom_call_target="tpu_custom_call", output_to_operand_aliasing={{0}: (10, {})} | custom-call | flops 9663676416 | bytes 31981568 | tf_op jit(solution)/shard_map/product/pallas_call | solution.py:51
  535.4 11.5 %product.17 = (f32[1152,8192]{1,0:T(8,128)}, f32[1,1024]{1,0:T(1,128)S(1)}, f32[1152,128]{1,0:T(8,128)S(1)}) custom-call(s32[8]{0:T(128)S(1)} %stack.35.place_ref, bf16[1152,4096]{1,0:T(8,128)(2,1)} %bitcast.25, bf16[256,2048]{1,0:T(8,128)(2,1)S(1)} %collective-permute-done.23.refs_0_, ...), custom_call_target="tpu_custom_call", output_to_operand_aliasing={{0}: (10, {})} | custom-call | flops 4831838208 | bytes 18350080 | tf_op jit(solution)/shard_map/product/pallas_call | solution.py:51
  621.1 47.2 %weight_step.1 = (f32[1152,8192]{1,0:T(8,128)}, bf16[1152,8192]{1,0:T(8,128)(2,1)}) custom-call(f32[1,1]{1,0:T(1,128)S(6)} %div.85.clip_ref, f32[1152,1]{1,0:T(8,128)S(1)} %broadcast_in_dim.16.row_ref, f32[1,8192]{1,0:T(1,128)S(1)} %maximum_rsqrt_fusion.col_ref, f32[1152,8192]{1,0:T(8,128)} %weight_ref.1, f32[1152,8192]{1,0:T(8,128)} %get-tuple-element.122.grad_ref), custom_call_target="tpu_custom_call" | custom-call | flops 47185920 | bytes 132120576 | tf_op jit(solution)/shard_map/weight_step/pallas_call | solution.py:92
  (244 shorter events, 177.5 us)
Async XLA Ops:
  0.6 161.2 %collective-permute-start.15 = (bf16[256,8192]{1,0:T(8,128)(2,1)}, bf16[256,8192]{1,0:T(8,128)(2,1)}, u32[]{:S(2)}, u32[]{:S(2)}) collective-permute-start(bf16[256,8192]{1,0:T(8,128)(2,1)} %refs_0_.7), channel_id=1, source_target_pairs={{0,4},{2,6},{4,0},{6,2},{1,5},{3,7},{5,1},{7,3},{8,12},{10,14},{12... | collective-permute-start | bytes 12582920 | tf_op jit(solution)/shard_map/ppermute | solution.py:116
  9.6 49.0 %collective-permute-start.19 = (bf16[256,2048]{1,0:T(8,128)(2,1)}, bf16[256,2048]{1,0:T(8,128)(2,1)S(1)}, u32[]{:S(2)}, u32[]{:S(2)}) collective-permute-start(bf16[256,2048]{1,0:T(8,128)(2,1)} %get-tuple-element.144), channel_id=1, source_target_pairs={{0,8},{8,16},{16,24},{24,0},{1,9},{9,17},{17,25},{25,1},{2,10},{10... | collective-permute-start | bytes 3145736 | tf_op jit(solution)/shard_map/ppermute | solution.py:116
  11.2 70.0 %collective-permute-start.10 = (bf16[256,2048]{1,0:T(8,128)(2,1)}, bf16[256,2048]{1,0:T(8,128)(2,1)S(1)}, u32[]{:S(2)}, u32[]{:S(2)}) collective-permute-start(bf16[256,2048]{1,0:T(8,128)(2,1)} %get-tuple-element.145), channel_id=1, source_target_pairs={{0,8},{8,16},{16,24},{24,0},{1,9},{9,17},{17,25},{25,1},{2,10},{10... | collective-permute-start | bytes 3145736 | tf_op jit(solution)/shard_map/ppermute | solution.py:116
  18.9 62.5 %collective-permute-start = (bf16[512,1152]{0,1:T(8,128)(2,1)S(1)}, bf16[512,1152]{0,1:T(8,128)(2,1)}, u32[]{:S(2)}, u32[]{:S(2)}) collective-permute-start(bf16[512,1152]{0,1:T(8,128)(2,1)S(1)} %copy.32), channel_id=1, source_target_pairs={{0,1},{1,0},{2,3},{3,2},{4,5},{5,4},{6,7},{7,6},{8,9},{9,8},{10,11... | collective-permute-start | bytes 3538952 | tf_op jit(solution)/shard_map/ppermute | solution.py:116
  36.2 70.3 %collective-permute-start.1 = (bf16[512,1152]{0,1:T(8,128)(2,1)}, bf16[512,1152]{0,1:T(8,128)(2,1)}, u32[]{:S(2)}, u32[]{:S(2)}) collective-permute-start(bf16[512,1152]{0,1:T(8,128)(2,1)} %copy.33), channel_id=1, source_target_pairs={{0,8},{8,16},{16,24},{24,0},{1,9},{9,17},{17,25},{25,1},{2,10},{10... | collective-permute-start | bytes 3538952 | tf_op jit(solution)/shard_map/ppermute | solution.py:116
  58.6 97.0 %collective-permute-start.3 = (bf16[512,1152]{0,1:T(8,128)(2,1)}, bf16[512,1152]{0,1:T(8,128)(2,1)}, u32[]{:S(2)}, u32[]{:S(2)}) collective-permute-start(bf16[512,1152]{0,1:T(8,128)(2,1)} %copy.34), channel_id=1, source_target_pairs={{0,16},{8,24},{16,0},{24,8},{1,17},{9,25},{17,1},{25,9},{2,18},{10... | collective-permute-start | bytes 3538952 | tf_op jit(solution)/shard_map/ppermute | solution.py:116
  81.1 76.1 %collective-permute-start.8 = (bf16[256,2048]{1,0:T(8,128)(2,1)}, bf16[256,2048]{1,0:T(8,128)(2,1)}, u32[]{:S(2)}, u32[]{:S(2)}) collective-permute-start(bf16[256,2048]{1,0:T(8,128)(2,1)} %collective-permute-done.7.refs_4_), channel_id=1, source_target_pairs={{0,4},{2,6},{4,0},{6,2},{1,5},{3,7},{5,1},{7,3},{8,12},{10,14},{12... | collective-permute-start | bytes 3145736 | tf_op jit(solution)/shard_map/ppermute | solution.py:116
  81.4 78.9 %collective-permute-start.11 = (bf16[256,2048]{1,0:T(8,128)(2,1)S(1)}, bf16[256,2048]{1,0:T(8,128)(2,1)}, u32[]{:S(2)}, u32[]{:S(2)}) collective-permute-start(bf16[256,2048]{1,0:T(8,128)(2,1)S(1)} %collective-permute-done.10.refs_4_), channel_id=1, source_target_pairs={{0,4},{2,6},{4,0},{6,2},{1,5},{3,7},{5,1},{7,3},{8,12},{10,14},{12... | collective-permute-start | bytes 3145736 | tf_op jit(solution)/shard_map/ppermute | solution.py:116
  106.5 55.3 %collective-permute-start.28 = (bf16[256,2048]{1,0:T(8,128)(2,1)S(1)}, bf16[256,2048]{1,0:T(8,128)(2,1)S(1)}, u32[]{:S(2)}, u32[]{:S(2)}) collective-permute-start(bf16[256,2048]{1,0:T(8,128)(2,1)S(1)} %collective-permute-done.19.refs_4_), channel_id=1, source_target_pairs={{0,4},{2,6},{4,0},{6,2},{1,5},{3,7},{5,1},{7,3},{8,12},{10,14},{12... | collective-permute-start | bytes 3145736 | tf_op jit(solution)/shard_map/ppermute | solution.py:116
  160.3 104.5 %collective-permute-start.14 = (bf16[256,8192]{1,0:T(8,128)(2,1)}, bf16[256,8192]{1,0:T(8,128)(2,1)S(1)}, u32[]{:S(2)}, u32[]{:S(2)}) collective-permute-start(bf16[256,8192]{1,0:T(8,128)(2,1)} %refs_0_.7), channel_id=1, source_target_pairs={{0,2},{2,0},{4,6},{6,4},{1,3},{3,1},{5,7},{7,5},{8,10},{10,8},{12,... | collective-permute-start | bytes 12582920 | tf_op jit(solution)/shard_map/ppermute | solution.py:120
  161.8 105.4 %collective-permute-start.16 = (bf16[256,8192]{1,0:T(8,128)(2,1)}, bf16[256,8192]{1,0:T(8,128)(2,1)S(1)}, u32[]{:S(2)}, u32[]{:S(2)}) collective-permute-start(bf16[256,8192]{1,0:T(8,128)(2,1)} %collective-permute-done.15.refs_2_), channel_id=1, source_target_pairs={{0,2},{2,0},{4,6},{6,4},{1,3},{3,1},{5,7},{7,5},{8,10},{10,8},{12,... | collective-permute-start | bytes 12582920 | tf_op jit(solution)/shard_map/ppermute | solution.py:120
  185.2 51.0 %collective-permute-start.6 = (bf16[512,1152]{0,1:T(8,128)(2,1)S(1)}, bf16[512,1152]{0,1:T(8,128)(2,1)S(1)}, u32[]{:S(2)}, u32[]{:S(2)}) collective-permute-start(bf16[512,1152]{0,1:T(8,128)(2,1)S(1)} %collective-permute-done.5), channel_id=1, source_target_pairs={{0,1},{1,0},{2,3},{3,2},{4,5},{5,4},{6,7},{7,6},{8,9},{9,8},{10,11... | collective-permute-start | bytes 3538952 | tf_op jit(solution)/shard_map/ppermute | solution.py:116
  187.3 48.9 %collective-permute-start.9 = (bf16[256,2048]{1,0:T(8,128)(2,1)S(1)}, bf16[256,2048]{1,0:T(8,128)(2,1)S(1)}, u32[]{:S(2)}, u32[]{:S(2)}) collective-permute-start(bf16[256,2048]{1,0:T(8,128)(2,1)S(1)} %copy-done.19), channel_id=1, source_target_pairs={{0,8},{8,16},{16,24},{24,0},{1,9},{9,17},{17,25},{25,1},{2,10},{10... | collective-permute-start | bytes 3145736 | tf_op jit(solution)/shard_map/ppermute | solution.py:116
  261.9 44.3 %collective-permute-start.33 = (bf16[256,2048]{1,0:T(8,128)(2,1)S(1)}, bf16[256,2048]{1,0:T(8,128)(2,1)S(1)}, u32[]{:S(2)}, u32[]{:S(2)}) collective-permute-start(bf16[256,2048]{1,0:T(8,128)(2,1)S(1)} %collective-permute-done.29.refs_0_), channel_id=1, source_target_pairs={{0,4},{2,6},{4,0},{6,2},{1,5},{3,7},{5,1},{7,3},{8,12},{10,14},{12... | collective-permute-start | bytes 3145736 | tf_op jit(solution)/shard_map/ppermute | solution.py:116
  264.8 42.4 %collective-permute-start.17 = (bf16[256,2048]{1,0:T(8,128)(2,1)S(1)}, bf16[256,2048]{1,0:T(8,128)(2,1)S(1)}, u32[]{:S(2)}, u32[]{:S(2)}) collective-permute-start(bf16[256,2048]{1,0:T(8,128)(2,1)S(1)} %collective-permute-done.10.refs_4_), channel_id=1, source_target_pairs={{0,2},{2,0},{4,6},{6,4},{1,3},{3,1},{5,7},{7,5},{8,10},{10,8},{12,... | collective-permute-start | bytes 3145736 | tf_op jit(solution)/shard_map/ppermute | solution.py:120
  264.8 59.6 %collective-permute-start.34 = (bf16[256,2048]{1,0:T(8,128)(2,1)S(1)}, bf16[256,2048]{1,0:T(8,128)(2,1)S(1)}, u32[]{:S(2)}, u32[]{:S(2)}) collective-permute-start(bf16[256,2048]{1,0:T(8,128)(2,1)S(1)} %collective-permute-done.19.refs_4_), channel_id=1, source_target_pairs={{0,2},{2,0},{4,6},{6,4},{1,3},{3,1},{5,7},{7,5},{8,10},{10,8},{12,... | collective-permute-start | bytes 3145736 | tf_op jit(solution)/shard_map/ppermute | solution.py:120
  267.3 39.9 %collective-permute-start.18 = (bf16[256,2048]{1,0:T(8,128)(2,1)}, bf16[256,2048]{1,0:T(8,128)(2,1)S(1)}, u32[]{:S(2)}, u32[]{:S(2)}) collective-permute-start(bf16[256,2048]{1,0:T(8,128)(2,1)} %collective-permute-done.11.refs_6_), channel_id=1, source_target_pairs={{0,2},{2,0},{4,6},{6,4},{1,3},{3,1},{5,7},{7,5},{8,10},{10,8},{12,... | collective-permute-start | bytes 3145736 | tf_op jit(solution)/shard_map/ppermute | solution.py:120
  287.8 36.0 %collective-permute-start.25 = (bf16[256,2048]{1,0:T(8,128)(2,1)S(1)}, bf16[256,2048]{1,0:T(8,128)(2,1)}, u32[]{:S(2)}, u32[]{:S(2)}) collective-permute-start(bf16[256,2048]{1,0:T(8,128)(2,1)S(1)} %collective-permute-done.19.refs_4_), channel_id=1, source_target_pairs={{0,8},{8,16},{16,24},{24,0},{1,9},{9,17},{17,25},{25,1},{2,10},{10... | collective-permute-start | bytes 3145736 | tf_op jit(solution)/shard_map/ppermute | solution.py:116
  307.2 33.3 %collective-permute-start.31 = (bf16[256,2048]{1,0:T(8,128)(2,1)S(1)}, bf16[256,2048]{1,0:T(8,128)(2,1)S(1)}, u32[]{:S(2)}, u32[]{:S(2)}) collective-permute-start(bf16[256,2048]{1,0:T(8,128)(2,1)S(1)} %collective-permute-done.9.refs_4_), channel_id=1, source_target_pairs={{0,2},{2,0},{4,6},{6,4},{1,3},{3,1},{5,7},{7,5},{8,10},{10,8},{12,... | collective-permute-start | bytes 3145736 | tf_op jit(solution)/shard_map/ppermute | solution.py:120
  307.2 33.3 %collective-permute-start.32 = (bf16[256,2048]{1,0:T(8,128)(2,1)S(1)}, bf16[256,2048]{1,0:T(8,128)(2,1)S(1)}, u32[]{:S(2)}, u32[]{:S(2)}) collective-permute-start(bf16[256,2048]{1,0:T(8,128)(2,1)S(1)} %collective-permute-done.20.refs_6_), channel_id=1, source_target_pairs={{0,2},{2,0},{4,6},{6,4},{1,3},{3,1},{5,7},{7,5},{8,10},{10,8},{12,... | collective-permute-start | bytes 3145736 | tf_op jit(solution)/shard_map/ppermute | solution.py:120
  340.4 50.3 %collective-permute-start.23 = (bf16[256,2048]{1,0:T(8,128)(2,1)S(1)}, bf16[256,2048]{1,0:T(8,128)(2,1)S(1)}, u32[]{:S(2)}, u32[]{:S(2)}) collective-permute-start(bf16[256,2048]{1,0:T(8,128)(2,1)S(1)} %collective-permute-done.9.refs_4_), channel_id=1, source_target_pairs={{0,8},{8,16},{16,24},{24,0},{1,9},{9,17},{17,25},{25,1},{2,10},{10... | collective-permute-start | bytes 3145736 | tf_op jit(solution)/shard_map/ppermute | solution.py:116
  356.6 55.4 %collective-permute-start.36 = (bf16[256,2048]{1,0:T(8,128)(2,1)S(1)}, bf16[256,2048]{1,0:T(8,128)(2,1)S(1)}, u32[]{:S(2)}, u32[]{:S(2)}) collective-permute-start(bf16[256,2048]{1,0:T(8,128)(2,1)S(1)} %collective-permute-done.29.refs_0_), channel_id=1, source_target_pairs={{0,8},{8,16},{16,24},{24,0},{1,9},{9,17},{17,25},{25,1},{2,10},{10... | collective-permute-start | bytes 3145736 | tf_op jit(solution)/shard_map/ppermute | solution.py:116
  368.3 45.3 %collective-permute-start.44 = (bf16[256,2048]{1,0:T(8,128)(2,1)S(1)}, bf16[256,2048]{1,0:T(8,128)(2,1)S(1)}, u32[]{:S(2)}, u32[]{:S(2)}) collective-permute-start(bf16[256,2048]{1,0:T(8,128)(2,1)S(1)} %collective-permute-done.43.refs_4_), channel_id=1, source_target_pairs={{0,4},{2,6},{4,0},{6,2},{1,5},{3,7},{5,1},{7,3},{8,12},{10,14},{12... | collective-permute-start | bytes 3145736 | tf_op jit(solution)/shard_map/ppermute | solution.py:116
  369.8 44.4 %collective-permute-start.46 = (bf16[256,2048]{1,0:T(8,128)(2,1)S(1)}, bf16[256,2048]{1,0:T(8,128)(2,1)S(1)}, u32[]{:S(2)}, u32[]{:S(2)}) collective-permute-start(bf16[256,2048]{1,0:T(8,128)(2,1)S(1)} %collective-permute-done.12.refs_0_), channel_id=1, source_target_pairs={{0,2},{2,0},{4,6},{6,4},{1,3},{3,1},{5,7},{7,5},{8,10},{10,8},{12,... | collective-permute-start | bytes 3145736 | tf_op jit(solution)/shard_map/ppermute | solution.py:120
  (79 other events, 1589.3 us)
